TPU v7x, 32 devices: a whole 2x2x4 slice. The times are simulated.
32 devices in a mesh: wide: 8 (over z, x), narrow: 4 (over y, core).
Axes of the slice: x: 2, y: 2, z: 4, core: 2. Of those that a mesh axis runs over, the one named last changes fastest.
Arguments:
- state: float32 [4, 512, 512], P('narrow'), may hold values from -1.5 to 1.5
- left_env: float32 [32, 4, 512, 512], P('wide', 'narrow')
- right_env: float32 [32, 4, 512, 512], P('wide', 'narrow')
- left_sizes: int32 [4], replicated, may hold values from 1 to 512, 1536 in all
- right_sizes: int32 [4], replicated, may hold values from 1 to 512, 1536 in all
- channel_charge: int32 [32], P('wide'), may hold values from 0 to 2
Outputs:
- lanczos_vector: float32 [4, 512, 512], P('narrow', 'wide')
- alpha: float32 [], replicated
Inputs may be any that keep to these rules, and one draw needn't show every extreme that they name: `left_sizes`: basis states of each left sector; they add up to 1536, and some sector has exactly 512. `right_sizes`: basis states of each right sector; they add up to 1536, and some sector has exactly 512. `channel_charge`: 0 lowers the sector by one, 1 keeps it, 2 raises it by one.
All inputs are finite; a program needn't handle non-finite values.
Results may differ from a plain program's by a relative error of at most 0.0003.
Values sent between devices are 32-bit elements; how exact they have to be, the bound alone decides.
No kernel may reach another device: no remote copies, remote signals or barrier semaphores. Data moves between devices by JAX's collectives and lax.ppermute only.
A program may use at most 64 MiB of HBM per device.

v0:
```python
import jax
import jax.numpy as jnp
from jax import lax
from jax.sharding import PartitionSpec as P


def with_halo(cells, sides, width):
    for axis, dim in sides:
        count = lax.axis_size(axis)
        ends = count - 1
        head = lax.slice_in_dim(cells, 0, width, axis=dim)
        tail = lax.slice_in_dim(cells, cells.shape[dim] - width, cells.shape[dim], axis=dim)
        cells = jnp.concatenate(
            [
                lax.ppermute(tail, axis, [(i, (i + 1) % count) for i in range(ends)]),
                cells,
                lax.ppermute(head, axis, [((i + 1) % count, i) for i in range(ends)]),
            ],
            axis=dim,
        )
    return cells


def valid_vector(sizes, sector, block):
    labels = jnp.arange(sizes.shape[0], dtype=jnp.int32)
    count = jnp.sum(jnp.where(labels == sector, sizes, 0))
    positions = jnp.arange(block, dtype=jnp.int32)
    return (positions < count).astype(jnp.float32)


def per_device(state, left_env, right_env, left_sizes, right_sizes, channel_charge):
    sec_local = state.shape[0]
    block = state.shape[1]
    chan_local = left_env.shape[0]
    n_wide = lax.axis_size("wide")
    band = block // n_wide
    narrow_pos = lax.axis_index("narrow")
    wide_pos = lax.axis_index("wide")
    first = narrow_pos * sec_local
    sec = 0
    rows_ok = valid_vector(left_sizes, first + sec, block)
    cols_ok = valid_vector(right_sizes, first + sec, block)
    own_masks = [state[sec] * rows_ok[:, None] * cols_ok[None, :]]
    psi = jnp.stack(own_masks)
    lmats = []
    rmats = []
    offsets = []
    for chan in range(chan_local):
        shift_by = channel_charge[chan] - 1
        sec = 0
        sector = first + sec
        source = sector - shift_by
        lmat = (
            left_env[chan, sec]
            * valid_vector(left_sizes, sector, block)[:, None]
            * valid_vector(left_sizes, source, block)[None, :]
        )
        rmat = (
            right_env[chan, sec]
            * valid_vector(right_sizes, sector, block)[:, None]
            * valid_vector(right_sizes, source, block)[None, :]
        )
        lmats.append(lmat)
        rmats.append(rmat)
        offsets.append(sec - shift_by + 1)
    extended = with_halo(psi, (("narrow", 0),), 1)
    inners = []
    for item in range(chan_local * sec_local):
        psi_src = lax.dynamic_index_in_dim(extended, offsets[item], 0, keepdims=False)
        inners.append(jnp.dot(lmats[item], psi_src, precision=lax.Precision.HIGHEST))
    sec = 0
    total = jnp.zeros((block, block), jnp.float32)
    for chan in range(chan_local):
        item = chan * sec_local + sec
        total = total + jnp.dot(inners[item], rmats[item].T, precision=lax.Precision.HIGHEST)
    sector_terms = [total]
    terms = jnp.stack(sector_terms)
    share = lax.psum_scatter(terms, "wide", scatter_dimension=1, tiled=True)
    psi_mine = lax.dynamic_slice_in_dim(psi, wide_pos * band, band, 1)
    denominator = jnp.sum(psi_mine * psi_mine)
    numerator = jnp.sum(psi_mine * share)
    numerator, denominator = lax.psum((numerator, denominator), ("wide", "narrow"))
    alpha = numerator / denominator
    return (share - alpha * psi_mine, alpha)


def solution(mesh):
    placed = (
        P("narrow", None, None),
        P("wide", "narrow", None, None),
        P("wide", "narrow", None, None),
        P(),
        P(),
        P("wide"),
    )
    return jax.shard_map(
        per_device,
        mesh=mesh,
        in_specs=placed,
        out_specs=(P("narrow", "wide", None), P()),
        check_vma=False,
    )
```

profile of v0, /device:TPU:0, one launch (start us, length us, event | category | flops | bytes accessed | tf_op | source)
XLA Modules:
  0.0 170.4 jit_solution(3171247605672984438)
XLA Ops:
  7.2 0.0 reduce-scatter.2.cloned.1.call-start
  7.2 1.4 fusion.84
  11.1 1.5 fusion.82
  12.7 0.6 fusion.62
  13.3 0.6 fusion.60
  13.9 1.4 multiply_multiply_fusion
  15.3 2.4 %collective-permute-start = (f32[1,512,512]{2,1,0:T(8,128)S(1)}, f32[1,512,512]{2,1,0:T(8,128)S(1)}, u32[]{:S(2)}, u32[]{:S(2)}) collective-permute-start(f32[1,512,512]{2,1,0:T(8,128)S(1)} %multiply_multiply_fusion), channel_id=1, source_target_pairs={{0,1},{1,2},{2,3},{4,5},{5,6},{6,7},{8,9},{9,10},{10,11},{12,13},{... | collective-permute-start | bytes 3145736 | tf_op jit(solution)/shard_map/ppermute | solution.py:15
  17.8 1.3 collective-permute-start.1
  19.1 0.0 copy-start.1
  19.1 0.8 fusion.61
  19.9 0.9 fusion.63
  20.7 0.6 fusion.64
  21.4 0.6 fusion.65
  21.9 0.6 fusion.66
  22.6 0.6 fusion.67
  23.1 0.6 fusion.68
  23.8 0.7 fusion.69
  24.5 0.0 collective-permute-done
  24.5 0.0 collective-permute-done.1
  24.5 0.3 pad_maximum_fusion
  24.8 0.0 copy-done.1
  24.8 1.9 %fusion.19 = f32[512,512]{1,0:T(8,128)S(1)} fusion(f32[3,512,512]{2,1,0:T(8,128)S(1)} %pad_maximum_fusion, s32[]{:T(128)S(6)} %select_n.58, f32[4,1,512,512]{3,2,1,0:T(8,128)S(1)} %copy-done.1, f32[512]{0:T(512)S(1)} %fusion.61, f32[512]{0:T(512)S(1)} %fusion.60), kind=kOutput, calls=%fused_computation.23 | convolution fusion | flops 1611137024 | bytes 3149828 | tf_op jit(solution)/shard_map/dot_general | solution.py:70
  26.7 0.0 copy-start
  26.8 1.9 %fusion.13 = f32[512,512]{1,0:T(8,128)S(1)} fusion(f32[3,512,512]{2,1,0:T(8,128)S(1)} %pad_maximum_fusion, s32[]{:T(128)S(6)} %select_n.61, f32[4,1,512,512]{3,2,1,0:T(8,128)S(1)} %copy-done.1, f32[512]{0:T(512)S(1)} %fusion.64, f32[512]{0:T(512)S(1)} %fusion.60), kind=kOutput, calls=%fused_computation.17 | convolution fusion | flops 1611137024 | bytes 3149828 | tf_op jit(solution)/shard_map/dot_general | solution.py:70
  28.7 1.9 %fusion.8 = f32[512,512]{1,0:T(8,128)S(1)} fusion(f32[3,512,512]{2,1,0:T(8,128)S(1)} %pad_maximum_fusion, s32[]{:T(128)S(6)} %select_n.64, f32[4,1,512,512]{3,2,1,0:T(8,128)S(1)} %copy-done.1, f32[512]{0:T(512)S(1)} %fusion.66, f32[512]{0:T(512)S(1)} %fusion.60), kind=kOutput, calls=%fused_computation.12 | convolution fusion | flops 1611137024 | bytes 3149828 | tf_op jit(solution)/shard_map/dot_general | solution.py:70
  30.6 1.9 %fusion.3 = f32[512,512]{1,0:T(8,128)S(1)} fusion(f32[3,512,512]{2,1,0:T(8,128)S(1)} %pad_maximum_fusion, s32[]{:T(128)S(6)} %select_n.67, f32[4,1,512,512]{3,2,1,0:T(8,128)S(1)} %copy-done.1, f32[512]{0:T(512)S(1)} %fusion.68, f32[512]{0:T(512)S(1)} %fusion.60), kind=kOutput, calls=%fused_computation.7 | convolution fusion | flops 1611137024 | bytes 3149828 | tf_op jit(solution)/shard_map/dot_general | solution.py:70
  32.5 0.0 copy-done
  32.5 2.0 %fusion.17 = f32[512,512]{1,0:T(8,128)S(1)} fusion(f32[512,512]{1,0:T(8,128)S(1)} %fusion.19, f32[4,1,512,512]{3,2,1,0:T(8,128)S(1)} %copy-done, f32[512]{0:T(512)S(1)} %fusion.63, f32[512]{0:T(512)S(1)} %fusion.62), kind=kOutput, calls=%fused_computation.22 | convolution fusion | flops 1611137024 | bytes 3149824 | tf_op jit(solution)/shard_map/dot_general | solution.py:75
  34.5 2.0 %convolution_add_fusion.2 = f32[512,512]{1,0:T(8,128)S(1)} fusion(f32[512,512]{1,0:T(8,128)S(1)} %fusion.17, f32[512,512]{1,0:T(8,128)S(1)} %fusion.13, f32[4,1,512,512]{3,2,1,0:T(8,128)S(1)} %copy-done, f32[512]{0:T(512)S(1)} %fusion.65, f32[512]{0:T(512)S(1)} %fusion.62), kind=kOutput, calls=%fused_computation.4 | convolution fusion | flops 1611399168 | bytes 4198400 | tf_op jit(solution)/shard_map/dot_general | solution.py:75
  36.5 2.0 %convolution_add_fusion.1 = f32[512,512]{1,0:T(8,128)S(1)} fusion(f32[512,512]{1,0:T(8,128)S(1)} %convolution_add_fusion.2, f32[512,512]{1,0:T(8,128)S(1)} %fusion.8, f32[4,1,512,512]{3,2,1,0:T(8,128)S(1)} %copy-done, f32[512]{0:T(512)S(1)} %fusion.67, f32[512]{0:T(512)S(1)} %fusion.62), kind=kOutput, calls=%fused_computation.3 | convolution fusion | flops 1611399168 | bytes 4198400 | tf_op jit(solution)/shard_map/dot_general | solution.py:75
  38.5 3.0 %fusion = f32[1,512,512]{2,1,0:T(8,128)} fusion(f32[512,512]{1,0:T(8,128)S(1)} %convolution_add_fusion.1, f32[512,512]{1,0:T(8,128)S(1)} %fusion.3, f32[4,1,512,512]{3,2,1,0:T(8,128)S(1)} %copy-done, f32[512]{0:T(512)S(1)} %fusion.69, f32[512]{0:T(512)S(1)} %fusion.62), kind=kOutput, calls=%fused_computation.2 | convolution fusion | flops 1611399168 | bytes 4198400 | tf_op jit(solution)/shard_map/dot_general | solution.py:75
  41.5 0.0 reduce-scatter.2.cloned.1.call-update
  41.6 0.1 dynamic-slice.5
  41.6 1.6 multiply_reduce_fusion
  43.3 74.2 %reduce-scatter.2.cloned.1.call-done = f32[1,64,512]{2,1,0:T(8,128)} async-done(((f32[1,512,512]{2,1,0:T(8,128)}), f32[1,64,512]{2,1,0:T(8,128)}) %reduce-scatter.2.cloned.1.call-update) | async-done | bytes 131088 | tf_op jit(solution)/shard_map/reduce_scatter | solution.py:78
  117.5 1.7 fusion.59
  119.2 40.2 %all-reduce = (f32[]{:T(128)}, f32[]{:T(128)}) all-reduce(f32[]{:T(128)} %fusion.59, f32[]{:T(128)} %multiply_reduce_fusion), channel_id=1, replica_groups=mesh['wide'=8,'narrow'=4] {'wide','narrow'}, use_global_device_ids=true, to_apply=%region_12.13 | all-reduce | flops 2 | bytes 16 | tf_op jit(solution)/shard_map/psum | solution.py:82
  160.7 1.7 %bitcast_subtract_fusion = f32[1,64,512]{2,1,0:T(8,128)} fusion(f32[1,64,512]{2,1,0:T(8,128)} %reduce-scatter.2.cloned.1.call-done, f32[512,512]{1,0:T(8,128)} %bitcast.63, s32[]{:T(128)S(6)} %select_n.69, f32[512]{0:T(512)S(1)} %fusion.62, f32[64]{0:T(128)S(1)} %dynamic-slice.5, f32[]{:T(128)} %div.3), kind=kLoop, calls=%fused_computation.65 | loop fusion | flops 131072 | bytes 395528 | tf_op jit(solution)/shard_map/sub | solution.py:84
Async XLA Ops:
  7.2 110.3 %reduce-scatter.2.cloned.1.call-start = ((), (), s32[]{:S(2)}) async-start(), calls=%async_computation.1 | async-start | bytes 1179648 | tf_op jit(solution)/shard_map/reduce_scatter | solution.py:78
  15.3 9.1 %collective-permute-start = (f32[1,512,512]{2,1,0:T(8,128)S(1)}, f32[1,512,512]{2,1,0:T(8,128)S(1)}, u32[]{:S(2)}, u32[]{:S(2)}) collective-permute-start(f32[1,512,512]{2,1,0:T(8,128)S(1)} %multiply_multiply_fusion), channel_id=1, source_target_pairs={{0,1},{1,2},{2,3},{4,5},{5,6},{6,7},{8,9},{9,10},{10,11},{12,13},{... | collective-permute-start | bytes 3145736 | tf_op jit(solution)/shard_map/ppermute | solution.py:15
  17.8 6.7 %collective-permute-start.1 = (f32[1,512,512]{2,1,0:T(8,128)S(1)}, f32[1,512,512]{2,1,0:T(8,128)S(1)}, u32[]{:S(2)}, u32[]{:S(2)}) collective-permute-start(f32[1,512,512]{2,1,0:T(8,128)S(1)} %multiply_multiply_fusion), channel_id=1, source_target_pairs={{1,0},{2,1},{3,2},{5,4},{6,5},{7,6},{9,8},{10,9},{11,10},{13,12},{... | collective-permute-start | bytes 3145736 | tf_op jit(solution)/shard_map/ppermute | solution.py:17
  19.1 5.7 %copy-start.1 = (f32[4,1,512,512]{3,2,1,0:T(8,128)S(1)}, f32[4,1,512,512]{3,2,1,0:T(8,128)}, u32[]{:S(2)}) copy-start(f32[4,1,512,512]{3,2,1,0:T(8,128)} %param.7) | copy-start | bytes 12582916
  26.7 5.8 %copy-start = (f32[4,1,512,512]{3,2,1,0:T(8,128)S(1)}, f32[4,1,512,512]{3,2,1,0:T(8,128)}, u32[]{:S(2)}) copy-start(f32[4,1,512,512]{3,2,1,0:T(8,128)} %param.8) | copy-start | bytes 12582916
Sparse Core Ops, SparseCore 0:
  41.7 75.7 reduce-scatter.1
where the time goes:
time: 171 us; the launch traced here: 170 us
  waiting for transfers between devices  74.2 us (43%)
  blocking collectives  40.2 us (24%)
  between operations  19.2 us (11%)
  matrix products  16.6 us (10%)
  other arithmetic  14.8 us (9%)
  starting transfers between devices  3.75 us (2%)
    reduce_scatter x1, waiting for transfers between devices, per_device(): share = lax.psum_scatter(terms, 'wide', scatter_dimension=1, tiled=True)  74.2 us
    psum x1, blocking collectives, per_device(): lax.psum((numerator, denominator), ('wide', 'narrow'))  40.2 us
    dot_general x4, matrix products, per_device(): jnp.dot(inners[item], rmats[item].T, precision=lax.Precision.HIGHEST)  8.98 us
    dot_general x4, matrix products, per_device(): jnp.dot(lmats[item], psi_src, precision=lax.Precision.HIGHEST)  7.67 us
    convert_element_type x10, other arithmetic, valid_vector(): return (positions < count).astype(jnp.float32)  6.57 us
  transfers between devices with their start and end apart: 3, of which 1 were waited for; matrix products, arithmetic and copies ran while one was open for 4% of the time, Pallas kernels for 0%

commit v1 on v0

v1 whole, which is shorter than its diff:
```python
import functools

import jax
import jax.numpy as jnp
from jax import lax
from jax.experimental import pallas as pl
from jax.experimental.pallas import tpu as pltpu
from jax.sharding import PartitionSpec as P

F32 = jnp.float32
BF16 = jnp.bfloat16
NN = (((1,), (0,)), ((), ()))
NT = (((1,), (1,)), ((), ()))
VMEM = pl.BlockSpec(memory_space=pltpu.VMEM)
SMEM = pl.BlockSpec(memory_space=pltpu.SMEM)
ANY = pl.BlockSpec(memory_space=pl.ANY)


def split(value):
    high = value.astype(BF16)
    low = (value - high.astype(F32)).astype(BF16)
    return high, low


def product(left, right, dims):
    (lh, ll), (rh, rl) = left, right
    dot = functools.partial(lax.dot_general, dimension_numbers=dims, preferred_element_type=F32)
    return dot(lh, rh) + (dot(lh, rl) + dot(ll, rh))


def size_at(sizes, sector):
    count = sizes.shape[0]
    inside = (sector >= 0) & (sector < count)
    return jnp.where(inside, sizes[jnp.clip(sector, 0, count - 1)], 0)


def keep(value, rows, cols, first_row=0):
    row = lax.broadcasted_iota(jnp.int32, value.shape, 0) + first_row
    col = lax.broadcasted_iota(jnp.int32, value.shape, 1)
    return jnp.where((row < rows) & (col < cols), value, 0.0)


def near_kernel(lsz, rsz, charge, own, near, left, right, total, lbuf, rbuf, psi_h, psi_l, sems):
    me = lax.axis_index("narrow")
    chans = left.shape[0]
    block = own.shape[0]
    partner = me + 1 - 2 * lax.rem(me, 2)

    def source(chan):
        return me - (charge[chan] - 1)

    def wanted(chan):
        src = source(chan)
        inside = (src >= 0) & (src < lsz.shape[0])
        return inside & ((src == me) | (src == partner))

    def copies(chan):
        return (
            pltpu.make_async_copy(right.at[chan, 0], rbuf.at[chan], sems.at[0, chan]),
            pltpu.make_async_copy(left.at[chan, 0], lbuf.at[chan], sems.at[1, chan]),
        )

    for chan in range(chans):

        @pl.when(wanted(chan))
        def _():
            for copy in copies(chan):
                copy.start()

    total[...] = jnp.zeros_like(total)
    for slot, (ref, sector) in enumerate(((own, me), (near, partner))):
        high, low = split(keep(ref[...], size_at(lsz, sector), size_at(rsz, sector)))
        psi_h[slot] = high
        psi_l[slot] = low

    def step(chan, carry):
        @pl.when(wanted(chan))
        def _():
            src = source(chan)
            slot = jnp.where(src == me, 0, 1)
            from_right, from_left = copies(chan)
            from_right.wait()
            rmat = split(keep(rbuf[chan], block, size_at(rsz, src)))
            y = split(product((psi_h[slot], psi_l[slot]), rmat, NT))
            from_left.wait()
            lmat = split(keep(lbuf[chan], block, size_at(lsz, src)))
            total[...] += product(lmat, y, NN)

        return carry

    lax.fori_loop(0, chans, step, 0)


def far_part(first, lsz, rsz, charge, far, left, right, total, lbuf, rbuf, sems):
    me = lax.axis_index("narrow")
    chans = left.shape[0]
    rows, block = far.shape
    other = me - 1 + 2 * lax.rem(me, 2)
    inside = (other >= 0) & (other < lsz.shape[0])

    def wanted(chan):
        return inside & (me - (charge[chan] - 1) == other)

    def copies(chan):
        return (
            pltpu.make_async_copy(right.at[chan, 0], rbuf.at[chan], sems.at[0, chan]),
            pltpu.make_async_copy(left.at[chan, 0, :, pl.ds(first, rows)], lbuf.at[chan], sems.at[1, chan]),
        )

    for chan in range(chans):

        @pl.when(wanted(chan))
        def _():
            for copy in copies(chan):
                copy.start()

    def step(chan, carry):
        @pl.when(wanted(chan))
        def _():
            lcount, rcount = size_at(lsz, other), size_at(rsz, other)
            psi = split(keep(far[...], lcount, rcount, first))
            from_right, from_left = copies(chan)
            from_right.wait()
            y = split(product(psi, split(keep(rbuf[chan], block, rcount)), NT))
            from_left.wait()
            lmat = split(keep(lbuf[chan], block, lcount - first))
            total[...] += product(lmat, y, NN)

        return carry

    lax.fori_loop(0, chans, step, 0)


def far_kernel(first, lsz, rsz, charge, far, left, right, before, total, lbuf, rbuf, sems):
    total[...] = before[...]
    far_part(first, lsz, rsz, charge, far, left, right, total, lbuf, rbuf, sems)


def last_kernel(first, lsz, rsz, charge, far, left, right, before, own, *rest):
    *outs, total, lbuf, rbuf, sems = rest
    total[...] = before[...]
    far_part(first, lsz, rsz, charge, far, left, right, total, lbuf, rbuf, sems)
    me = lax.axis_index("narrow")
    rows, cols = size_at(lsz, me), size_at(rsz, me)
    hpsi = keep(total[...], rows, cols)
    total[...] = hpsi
    numerator = jnp.sum(keep(own[...], rows, cols) * hpsi)
    here = lax.axis_index("wide")
    block = own.shape[0]
    band = block // len(outs)
    for shift, out in enumerate(outs):
        start = pl.multiple_of((here ^ shift) * band, band)
        out[:band, :] = total[pl.ds(start, band), :]
        out[band:, :] = jnp.full((out.shape[0] - band, out.shape[1]), numerator, F32)


def gather_kernel(lsz, rsz, own, *rest):
    *parts, share, sums = rest
    band = share.shape[0]
    whole = parts[0][...]
    for part in parts[1:]:
        whole += part[...]
    share[...] = whole[:band]
    me = lax.axis_index("narrow")
    psi = keep(own[...], size_at(lsz, me), size_at(rsz, me))
    denominator = jnp.sum(psi * psi)
    row = lax.broadcasted_iota(jnp.int32, sums.shape, 0)
    sums[...] = jnp.where(row == 0, whole[band : band + 8, : sums.shape[1]], denominator)


def final_kernel(lsz, rsz, own, share, *rest):
    *sums, out, alpha = rest
    both = sums[0][...]
    for more in sums[1:]:
        both += more[...]
    ratio = both[0:1, :] / both[1:2, :]
    me = lax.axis_index("narrow")
    band = share.shape[0]
    start = pl.multiple_of(lax.axis_index("wide") * band, band)
    psi = keep(own[pl.ds(start, band), :], size_at(lsz, me), size_at(rsz, me), start)
    out[...] = share[...] - jnp.concatenate([ratio] * (psi.shape[1] // ratio.shape[1]), axis=1) * psi
    alpha[...] = ratio


def exchange(value, axis, shift):
    count = lax.axis_size(axis)
    return lax.ppermute(value, axis, [(i, i ^ shift) for i in range(count)])


def per_device(state, left_env, right_env, left_sizes, right_sizes, channel_charge):
    chans, _, block, _ = left_env.shape
    n_wide, n_narrow = lax.axis_size("wide"), lax.axis_size("narrow")
    band = block // n_wide
    own = state[0]
    params = pltpu.CompilerParams(vmem_limit_bytes=40 * 2**20)
    scalars = (left_sizes, right_sizes, channel_charge)
    square = jax.ShapeDtypeStruct((block, block), F32)

    ends = [(0, 0), (n_narrow - 1, n_narrow - 1)]
    across = [pair for k in range(1, n_narrow - 1, 2) for pair in ((k, k + 1), (k + 1, k))]
    near = exchange(own, "narrow", 1)
    chunks = 2
    rows = block // chunks
    fars = [lax.ppermute(own[i * rows : (i + 1) * rows], "narrow", across + ends) for i in range(chunks)]

    total = pl.pallas_call(
        near_kernel,
        out_shape=square,
        in_specs=[SMEM] * 3 + [VMEM] * 2 + [ANY] * 2,
        out_specs=VMEM,
        scratch_shapes=[
            pltpu.VMEM((chans, block, block), F32),
            pltpu.VMEM((chans, block, block), F32),
            pltpu.VMEM((2, block, block), BF16),
            pltpu.VMEM((2, block, block), BF16),
            pltpu.SemaphoreType.DMA((2, chans)),
        ],
        compiler_params=params,
        name="near",
    )(*scalars, own, near, left_env, right_env)

    far_scratch = [
        pltpu.VMEM((chans, block, rows), F32),
        pltpu.VMEM((chans, block, block), F32),
        pltpu.SemaphoreType.DMA((2, chans)),
    ]
    for i in range(chunks - 1):
        total = pl.pallas_call(
            functools.partial(far_kernel, i * rows),
            out_shape=square,
            in_specs=[SMEM] * 3 + [VMEM] + [ANY] * 2 + [VMEM],
            out_specs=VMEM,
            scratch_shapes=far_scratch,
            compiler_params=params,
            name="far",
        )(*scalars, fars[i], left_env, right_env, total)
    message = jax.ShapeDtypeStruct((band + 8, block), F32)
    bands = pl.pallas_call(
        functools.partial(last_kernel, (chunks - 1) * rows),
        out_shape=[message] * n_wide,
        in_specs=[SMEM] * 3 + [VMEM] + [ANY] * 2 + [VMEM] * 2,
        out_specs=[VMEM] * n_wide,
        scratch_shapes=[pltpu.VMEM((block, block), F32)] + far_scratch,
        compiler_params=params,
        name="last",
    )(*scalars, fars[-1], left_env, right_env, total, own)

    parts = [bands[0]] + [exchange(bands[s], "wide", s) for s in range(n_wide - 1, 0, -1)]
    small = jax.ShapeDtypeStruct((8, 128), F32)
    share, sums = pl.pallas_call(
        gather_kernel,
        out_shape=[jax.ShapeDtypeStruct((band, block), F32), small],
        in_specs=[SMEM] * 2 + [VMEM] * (1 + n_wide),
        out_specs=[VMEM, VMEM],
        compiler_params=params,
        name="gather",
    )(left_sizes, right_sizes, own, *parts)
    every = [sums] + [exchange(sums, "narrow", s) for s in range(1, n_narrow)]
    out, alpha = pl.pallas_call(
        final_kernel,
        out_shape=[jax.ShapeDtypeStruct((band, block), F32), jax.ShapeDtypeStruct((1, 128), F32)],
        in_specs=[SMEM] * 2 + [VMEM] * (2 + len(every)),
        out_specs=[VMEM, VMEM],
        compiler_params=params,
        name="final",
    )(left_sizes, right_sizes, own, share, *every)
    return out[None], alpha[0, 0]


def solution(mesh):
    placed = (
        P("narrow", None, None),
        P("wide", "narrow", None, None),
        P("wide", "narrow", None, None),
        P(),
        P(),
        P("wide"),
    )
    return jax.shard_map(
        per_device,
        mesh=mesh,
        in_specs=placed,
        out_specs=(P("narrow", "wide", None), P()),
        check_vma=False,
    )
```

time: 171 us -> 60.1 us (0.35)
  waiting for transfers between devices: 74.2 us -> 18.3 us
  blocking collectives: 40.2 us -> 0 us
  between operations: 19.2 us -> 0.77 us
  matrix products: 16.6 us -> 0 us
  starting transfers between devices: 3.75 us -> 19.4 us
  other arithmetic: 14.8 us -> 0 us
  Pallas kernels: 0 us -> 12 us
  local copies, waits for them, and re-layouts: 1.51 us -> 8.84 us
    reduce_scatter x1 -> x0, waiting for transfers between devices: 74.2 us -> none  [per_device(): share = lax.psum_scatter(terms, 'wide', scatter_dimension=1, tiled=True)]
    psum x1 -> x0, blocking collectives: 40.2 us -> none  [per_device(): lax.psum((numerator, denominator), ('wide', 'narrow'))]
    ppermute x2 -> x13, waiting for transfers between devices: 0.01 us -> 18.3 us  [the longest x11 18.3 us: exchange(): return lax.ppermute(value, axis, [(i, i ^ shift) for i in range(count)])]
    dot_general x8 -> x0, matrix products: 16.6 us -> none  [the longest x4 8.98 us: per_device(): jnp.dot(inners[item], rmats[item].T, precision=lax.Precision.HIGHEST)]
    ppermute x2 -> x13, starting transfers between devices: 3.72 us -> 19.4 us  [the longest x11 18 us: exchange(): return lax.ppermute(value, axis, [(i, i ^ shift) for i in range(count)])]
    pallas_call x0 -> x5, Pallas kernels: none -> 12 us  [the longest x1 7.75 us: per_device(): pl.pallas_call(near_kernel, out_shape=square, in_specs=[SMEM] * 3 + [VMEM...]
    unnamed x4 -> x18, local copies, waits for them, and re-layouts: 0.01 us -> 7.57 us
    convert_element_type x10 -> x0, other arithmetic: 6.57 us -> none  [valid_vector(): return (positions < count).astype(jnp.float32)]
  transfers between devices with their start and end apart: 3 -> 13, of which waited for: 1 -> 4; matrix products, arithmetic and copies ran while one was open for 4% -> 2% of each run, Pallas kernels for 0% -> 14%
where the time goes in v1:
time: 60.1 us; the launch traced here: 59.4 us
  starting transfers between devices  19.4 us (32%)
  waiting for transfers between devices  18.3 us (30%)
  Pallas kernels  12 us (20%)
  local copies, waits for them, and re-layouts  8.84 us (15%)
  between operations  0.77 us (1%)
    ppermute x11, waiting for transfers between devices, exchange(): return lax.ppermute(value, axis, [(i, i ^ shift) for i in range(count)])  18.3 us
    ppermute x11, starting transfers between devices, exchange(): return lax.ppermute(value, axis, [(i, i ^ shift) for i in range(count)])  18 us
    pallas_call x1, Pallas kernels, per_device(): pl.pallas_call(near_kernel, out_shape=square, in_specs=[SMEM] * 3 + [VMEM...  7.75 us
    unnamed x18, local copies, waits for them, and re-layouts  7.57 us
    ppermute x2, starting transfers between devices, per_device(): lax.ppermute(own[i * rows:(i + 1) * rows], 'narrow', across + ends)  1.39 us
    pallas_call x1, Pallas kernels, per_device(): pl.pallas_call(functools.partial(last_kernel, (chunks - 1) * rows), out_s...  1.28 us
    slice x1, local copies, waits for them, and re-layouts, per_device(): own[i * rows:(i + 1) * rows]  1.27 us
    pallas_call x1, Pallas kernels, per_device(): pl.pallas_call(final_kernel, out_shape=[jax.ShapeDtypeStruct((band, block...  1.24 us
  transfers between devices with their start and end apart: 13, of which 4 were waited for; matrix products, arithmetic and copies ran while one was open for 2% of the time, Pallas kernels for 14%

profile of v1, /device:TPU:0, one launch (start us, length us, event | category | flops | bytes accessed | tf_op | source)
XLA Modules:
  0.0 59.4 jit_solution(12104406579834847425)
XLA Ops:
  0.6 0.5 collective-permute-start.2
  1.1 1.3 %slice_bitcast_fusion = (f32[256,512]{1,0:T(8,128)S(1)}, f32[256,512]{1,0:T(8,128)S(1)}) fusion(f32[1,512,512]{2,1,0:T(8,128)} %param.6), kind=kLoop, calls=%fused_computation | loop fusion | bytes 2097152 | tf_op jit(solution)/shard_map/slice | solution.py:204
  2.4 0.7 %collective-permute-start.1 = (f32[256,512]{1,0:T(8,128)S(1)}, f32[256,512]{1,0:T(8,128)S(1)}, u32[]{:S(2)}, u32[]{:S(2)}) collective-permute-start(f32[256,512]{1,0:T(8,128)S(1)} %get-tuple-element.26), channel_id=1, source_target_pairs={{1,2},{2,1},{0,0},{3,3},{5,6},{6,5},{4,4},{7,7},{9,10},{10,9},{8,8... | collective-permute-start | bytes 1572872 | tf_op jit(solution)/shard_map/ppermute | solution.py:204
  3.1 0.7 %collective-permute-start = (f32[256,512]{1,0:T(8,128)S(1)}, f32[256,512]{1,0:T(8,128)S(1)}, u32[]{:S(2)}, u32[]{:S(2)}) collective-permute-start(f32[256,512]{1,0:T(8,128)S(1)} %get-tuple-element.27), channel_id=1, source_target_pairs={{1,2},{2,1},{0,0},{3,3},{5,6},{6,5},{4,4},{7,7},{9,10},{10,9},{8,8... | collective-permute-start | bytes 1572872 | tf_op jit(solution)/shard_map/ppermute | solution.py:204
  3.8 0.0 collective-permute-done.2.near
  3.8 0.0 copy-start
  3.8 2.2 %copy-done = f32[4,1,512,512]{3,2,1,0:T(8,128)S(1)} copy-done((f32[4,1,512,512]{3,2,1,0:T(8,128)S(1)}, f32[4,1,512,512]{3,2,1,0:T(8,128)}, u32[]{:S(2)}) %copy-start) | copy-done | bytes 4194328
  6.0 0.0 copy-start.2
  6.0 2.2 %copy-done.2 = f32[4,1,512,512]{3,2,1,0:T(8,128)S(1)} copy-done((f32[4,1,512,512]{3,2,1,0:T(8,128)S(1)}, f32[4,1,512,512]{3,2,1,0:T(8,128)}, u32[]{:S(2)}) %copy-start.2) | copy-done | bytes 4194328
  8.2 0.0 copy-start.4
  8.2 1.2 %copy-done.4 = f32[1,512,512]{2,1,0:T(8,128)S(1)} copy-done((f32[1,512,512]{2,1,0:T(8,128)S(1)}, f32[1,512,512]{2,1,0:T(8,128)}, u32[]{:S(2)}) %copy-start.4) | copy-done | bytes 1048600
  9.4 0.0 copy-start.6
  9.4 0.7 %copy-done.6 = s32[4]{0:T(128)S(1)} copy-done((s32[4]{0:T(128)S(1)}, s32[4]{0:T(128)}, u32[]{:S(2)}) %copy-start.6) | copy-done | bytes 40
  10.1 0.0 copy-start.7
  10.1 0.7 %copy-done.7 = s32[4]{0:T(128)S(1)} copy-done((s32[4]{0:T(128)S(1)}, s32[4]{0:T(128)}, u32[]{:S(2)}) %copy-start.7) | copy-done | bytes 40
  10.7 0.0 copy-start.8
  10.8 0.7 %copy-done.8 = s32[4]{0:T(128)S(1)} copy-done((s32[4]{0:T(128)S(1)}, s32[4]{0:T(128)}, u32[]{:S(2)}) %copy-start.8) | copy-done | bytes 40
  11.4 7.8 %near.1.before = f32[512,512]{1,0:T(8,128)S(1)} custom-call(s32[4]{0:T(128)S(1)} %copy-done.6, s32[4]{0:T(128)S(1)} %copy-done.7, s32[4]{0:T(128)S(1)} %copy-done.8, f32[512,512]{1,0:T(8,128)S(1)} %bitcast.9, f32[512,512]{1,0:T(8,128)S(1)} %collective-permute-done.2.near, f32[4,1,512,512]{3,2,1,0:T(8,128)S(1)} %copy-done, f32[4,1,512,512]{3,2,1,0:T(8,128)S(1)} %copy-done.2), custom_call_target="tpu_custom_call" | custom-call | tf_op jit(solution)/shard_map/near/pallas_call | solution.py:206
  19.2 0.0 collective-permute-done.1.far
  19.2 0.0 copy-done.1
  19.2 0.0 copy-done.3
  19.2 0.8 %far.1.before = f32[512,512]{1,0:T(8,128)S(1)} custom-call(s32[4]{0:T(128)S(1)} %copy-done.6, s32[4]{0:T(128)S(1)} %copy-done.7, s32[4]{0:T(128)S(1)} %copy-done.8, f32[256,512]{1,0:T(8,128)S(1)} %collective-permute-done.1.far, f32[4,1,512,512]{3,2,1,0:T(8,128)S(1)} %copy-done.1, f32[4,1,512,512]{3,2,1,0:T(8,128)S(1)} %copy-done.3, f32[512,512]{1,0:T(8,128)S(1)} %near.1.before), custom_call_target="tpu_custom_call" | custom-call | tf_op jit(solution)/shard_map/far/pallas_call | solution.py:228
  20.0 0.0 copy-start.5
  20.0 0.0 collective-permute-done.far
  20.0 1.3 %last.1 = (f32[72,512]{1,0:T(8,128)S(1)}, f32[72,512]{1,0:T(8,128)S(1)}, f32[72,512]{1,0:T(8,128)S(1)}, f32[72,512]{1,0:T(8,128)S(1)}, f32[72,512]{1,0:T(8,128)S...) custom-call(s32[4]{0:T(128)S(1)} %copy-done.6, s32[4]{0:T(128)S(1)} %copy-done.7, ...), custom_call_target="tpu_custom_call" | custom-call | tf_op jit(solution)/shard_map/last/pallas_call | solution.py:238
  21.3 5.8 %collective-permute-start.3 = (f32[72,512]{1,0:T(8,128)S(1)}, f32[72,512]{1,0:T(8,128)S(1)}, u32[]{:S(2)}, u32[]{:S(2)}) collective-permute-start(f32[72,512]{1,0:T(8,128)S(1)} %get-tuple-element.15), channel_id=1, source_target_pairs={{0,28},{4,24},{8,20},{12,16},{16,12},{20,8},{24,4},{28,0},{1,29},{... | collective-permute-start | bytes 442376 | tf_op jit(solution)/shard_map/ppermute | solution.py:187
  27.0 0.2 collective-permute-start.4
  27.3 0.8 %collective-permute-start.5 = (f32[72,512]{1,0:T(8,128)S(1)}, f32[72,512]{1,0:T(8,128)S(1)}, u32[]{:S(2)}, u32[]{:S(2)}) collective-permute-start(f32[72,512]{1,0:T(8,128)S(1)} %get-tuple-element.17), channel_id=1, source_target_pairs={{0,20},{4,16},{8,28},{12,24},{16,4},{20,0},{24,12},{28,8},{1,21},{... | collective-permute-start | bytes 442376 | tf_op jit(solution)/shard_map/ppermute | solution.py:187
  28.0 2.0 %collective-permute-start.6 = (f32[72,512]{1,0:T(8,128)S(1)}, f32[72,512]{1,0:T(8,128)S(1)}, u32[]{:S(2)}, u32[]{:S(2)}) collective-permute-start(f32[72,512]{1,0:T(8,128)S(1)} %get-tuple-element.18), channel_id=1, source_target_pairs={{0,16},{4,20},{8,24},{12,28},{16,0},{20,4},{24,8},{28,12},{1,17},{... | collective-permute-start | bytes 442376 | tf_op jit(solution)/shard_map/ppermute | solution.py:187
  30.1 2.3 %collective-permute-start.7 = (f32[72,512]{1,0:T(8,128)S(1)}, f32[72,512]{1,0:T(8,128)S(1)}, u32[]{:S(2)}, u32[]{:S(2)}) collective-permute-start(f32[72,512]{1,0:T(8,128)S(1)} %get-tuple-element.19), channel_id=1, source_target_pairs={{0,12},{4,8},{8,4},{12,0},{16,28},{20,24},{24,20},{28,16},{1,13},{... | collective-permute-start | bytes 442376 | tf_op jit(solution)/shard_map/ppermute | solution.py:187
  32.3 0.0 collective-permute-done.3.rest_1_
  32.3 0.8 %collective-permute-start.8 = (f32[72,512]{1,0:T(8,128)S(1)}, f32[72,512]{1,0:T(8,128)S(1)}, u32[]{:S(2)}, u32[]{:S(2)}) collective-permute-start(f32[72,512]{1,0:T(8,128)S(1)} %get-tuple-element.20), channel_id=1, source_target_pairs={{0,8},{4,12},{8,0},{12,4},{16,24},{20,28},{24,16},{28,20},{1,9},{5... | collective-permute-start | bytes 442376 | tf_op jit(solution)/shard_map/ppermute | solution.py:187
  33.1 1.0 %collective-permute-done.4.rest_2_ = f32[72,512]{1,0:T(8,128)S(1)} collective-permute-done((f32[72,512]{1,0:T(8,128)S(1)}, f32[72,512]{1,0:T(8,128)S(1)}, u32[]{:S(2)}, u32[]{:S(2)}) %collective-permute-start.4) | collective-permute-done | bytes 147488 | tf_op jit(solution)/shard_map/ppermute | solution.py:187
  34.1 0.5 collective-permute-start.9
  34.6 10.2 %collective-permute-done.5.rest_3_ = f32[72,512]{1,0:T(8,128)S(1)} collective-permute-done((f32[72,512]{1,0:T(8,128)S(1)}, f32[72,512]{1,0:T(8,128)S(1)}, u32[]{:S(2)}, u32[]{:S(2)}) %collective-permute-start.5) | collective-permute-done | bytes 147488 | tf_op jit(solution)/shard_map/ppermute | solution.py:187
  44.8 5.6 %collective-permute-done.6.rest_4_ = f32[72,512]{1,0:T(8,128)S(1)} collective-permute-done((f32[72,512]{1,0:T(8,128)S(1)}, f32[72,512]{1,0:T(8,128)S(1)}, u32[]{:S(2)}, u32[]{:S(2)}) %collective-permute-start.6) | collective-permute-done | bytes 147488 | tf_op jit(solution)/shard_map/ppermute | solution.py:187
  50.5 0.0 collective-permute-done.7.rest_5_
  50.5 0.0 collective-permute-done.8.rest_6_
  50.5 0.0 collective-permute-done.9.rest_7_
  50.5 0.0 copy-done.5
  50.5 1.0 %gather.1 = (f32[64,512]{1,0:T(8,128)S(1)}, f32[8,128]{1,0:T(8,128)S(1)}) custom-call(s32[4]{0:T(128)S(1)} %copy-done.6, s32[4]{0:T(128)S(1)} %copy-done.7, f32[512,512]{1,0:T(8,128)S(1)} %bitcast.11, f32[72,512]{1,0:T(8,128)S(1)} %get-tuple-element.14.rest_0_, f32[72,512]{1,0:T(8,128)S(1)} %collective-permute-done.3.rest_1_, ...), custom_call_target="tpu_custom_call" | custom-call | tf_op jit(solution)/shard_map/gather/pallas_call | solution.py:250
  51.5 0.1 collective-permute-start.12
  51.6 5.0 %collective-permute-start.11 = (f32[8,128]{1,0:T(8,128)S(1)}, f32[8,128]{1,0:T(8,128)S(1)}, u32[]{:S(2)}, u32[]{:S(2)}) collective-permute-start(f32[8,128]{1,0:T(8,128)S(1)} %get-tuple-element.23.rest_0_), channel_id=1, source_target_pairs={{0,2},{1,3},{2,0},{3,1},{4,6},{5,7},{6,4},{7,5},{8,10},{9,11},{10,... | collective-permute-start | bytes 12296 | tf_op jit(solution)/shard_map/ppermute | solution.py:187
  56.6 0.0 collective-permute-start.10
  56.6 0.0 collective-permute-done.12.rest_3_
  56.6 1.5 %collective-permute-done.11.rest_2_ = f32[8,128]{1,0:T(8,128)S(1)} collective-permute-done((f32[8,128]{1,0:T(8,128)S(1)}, f32[8,128]{1,0:T(8,128)S(1)}, u32[]{:S(2)}, u32[]{:S(2)}) %collective-permute-start.11) | collective-permute-done | bytes 4128 | tf_op jit(solution)/shard_map/ppermute | solution.py:187
  58.2 0.0 collective-permute-done.10.rest_1_
  58.2 1.2 %final.1 = (f32[64,512]{1,0:T(8,128)}, f32[1,128]{1,0:T(1,128)}) custom-call(s32[4]{0:T(128)S(1)} %copy-done.6, s32[4]{0:T(128)S(1)} %copy-done.7, f32[512,512]{1,0:T(8,128)S(1)} %bitcast.12, f32[64,512]{1,0:T(8,128)S(1)} %get-tuple-element.22.share, f32[8,128]{1,0:T(8,128)S(1)} %get-tuple-element.23.rest_0_, f32[8,128]{1,0:T(8,128)S(1)} %collective-permute-done.10.rest_1_, ...), custom_call_target="tpu_custom_call" | custom-call | tf_op jit(solution)/shard_map/final/pallas_call | solution.py:259
  (2 shorter events, 0.0 us)
Async XLA Ops:
  0.6 3.2 %collective-permute-start.2 = (f32[512,512]{1,0:T(8,128)}, f32[512,512]{1,0:T(8,128)S(1)}, u32[]{:S(2)}, u32[]{:S(2)}) collective-permute-start(f32[512,512]{1,0:T(8,128)} %bitcast.8), channel_id=1, source_target_pairs={{0,1},{1,0},{2,3},{3,2},{4,5},{5,4},{6,7},{7,6},{8,9},{9,8},{10,11... | collective-permute-start | bytes 3145736 | tf_op jit(solution)/shard_map/ppermute | solution.py:187
  2.4 16.8 %collective-permute-start.1 = (f32[256,512]{1,0:T(8,128)S(1)}, f32[256,512]{1,0:T(8,128)S(1)}, u32[]{:S(2)}, u32[]{:S(2)}) collective-permute-start(f32[256,512]{1,0:T(8,128)S(1)} %get-tuple-element.26), channel_id=1, source_target_pairs={{1,2},{2,1},{0,0},{3,3},{5,6},{6,5},{4,4},{7,7},{9,10},{10,9},{8,8... | collective-permute-start | bytes 1572872 | tf_op jit(solution)/shard_map/ppermute | solution.py:204
  3.1 16.9 %collective-permute-start = (f32[256,512]{1,0:T(8,128)S(1)}, f32[256,512]{1,0:T(8,128)S(1)}, u32[]{:S(2)}, u32[]{:S(2)}) collective-permute-start(f32[256,512]{1,0:T(8,128)S(1)} %get-tuple-element.27), channel_id=1, source_target_pairs={{1,2},{2,1},{0,0},{3,3},{5,6},{6,5},{4,4},{7,7},{9,10},{10,9},{8,8... | collective-permute-start | bytes 1572872 | tf_op jit(solution)/shard_map/ppermute | solution.py:204
  3.8 2.2 %copy-start = (f32[4,1,512,512]{3,2,1,0:T(8,128)S(1)}, f32[4,1,512,512]{3,2,1,0:T(8,128)}, u32[]{:S(2)}) copy-start(f32[4,1,512,512]{3,2,1,0:T(8,128)} %left.5) | copy-start | bytes 12582916
  6.0 2.2 %copy-start.2 = (f32[4,1,512,512]{3,2,1,0:T(8,128)S(1)}, f32[4,1,512,512]{3,2,1,0:T(8,128)}, u32[]{:S(2)}) copy-start(f32[4,1,512,512]{3,2,1,0:T(8,128)} %right.5) | copy-start | bytes 12582916
  8.2 1.2 %copy-start.4 = (f32[1,512,512]{2,1,0:T(8,128)S(1)}, f32[1,512,512]{2,1,0:T(8,128)}, u32[]{:S(2)}) copy-start(f32[1,512,512]{2,1,0:T(8,128)} %param.6) | copy-start | bytes 3145732
  9.4 0.7 %copy-start.6 = (s32[4]{0:T(128)S(1)}, s32[4]{0:T(128)}, u32[]{:S(2)}) copy-start(s32[4]{0:T(128)} %lsz.9) | copy-start | bytes 52
  10.1 0.7 %copy-start.7 = (s32[4]{0:T(128)S(1)}, s32[4]{0:T(128)}, u32[]{:S(2)}) copy-start(s32[4]{0:T(128)} %rsz.9) | copy-start | bytes 52
  10.7 0.7 %copy-start.8 = (s32[4]{0:T(128)S(1)}, s32[4]{0:T(128)}, u32[]{:S(2)}) copy-start(s32[4]{0:T(128)} %charge.5) | copy-start | bytes 52
  11.4 7.8 %copy-start.1 = (f32[4,1,512,512]{3,2,1,0:T(8,128)S(1)}, f32[4,1,512,512]{3,2,1,0:T(8,128)}, u32[]{:S(2)}) copy-start(f32[4,1,512,512]{3,2,1,0:T(8,128)} %left.5) | copy-start | bytes 12582916
  11.4 7.8 %copy-start.3 = (f32[4,1,512,512]{3,2,1,0:T(8,128)S(1)}, f32[4,1,512,512]{3,2,1,0:T(8,128)}, u32[]{:S(2)}) copy-start(f32[4,1,512,512]{3,2,1,0:T(8,128)} %right.5) | copy-start | bytes 12582916
  20.0 30.5 %copy-start.5 = (f32[1,512,512]{2,1,0:T(8,128)S(1)}, f32[1,512,512]{2,1,0:T(8,128)}, u32[]{:S(2)}) copy-start(f32[1,512,512]{2,1,0:T(8,128)} %param.6) | copy-start | bytes 3145732
  21.3 11.0 %collective-permute-start.3 = (f32[72,512]{1,0:T(8,128)S(1)}, f32[72,512]{1,0:T(8,128)S(1)}, u32[]{:S(2)}, u32[]{:S(2)}) collective-permute-start(f32[72,512]{1,0:T(8,128)S(1)} %get-tuple-element.15), channel_id=1, source_target_pairs={{0,28},{4,24},{8,20},{12,16},{16,12},{20,8},{24,4},{28,0},{1,29},{... | collective-permute-start | bytes 442376 | tf_op jit(solution)/shard_map/ppermute | solution.py:187
  27.0 7.0 %collective-permute-start.4 = (f32[72,512]{1,0:T(8,128)S(1)}, f32[72,512]{1,0:T(8,128)S(1)}, u32[]{:S(2)}, u32[]{:S(2)}) collective-permute-start(f32[72,512]{1,0:T(8,128)S(1)} %get-tuple-element.16), channel_id=1, source_target_pairs={{0,24},{4,28},{8,16},{12,20},{16,8},{20,12},{24,0},{28,4},{1,25},{... | collective-permute-start | bytes 442376 | tf_op jit(solution)/shard_map/ppermute | solution.py:187
  27.3 17.5 %collective-permute-start.5 = (f32[72,512]{1,0:T(8,128)S(1)}, f32[72,512]{1,0:T(8,128)S(1)}, u32[]{:S(2)}, u32[]{:S(2)}) collective-permute-start(f32[72,512]{1,0:T(8,128)S(1)} %get-tuple-element.17), channel_id=1, source_target_pairs={{0,20},{4,16},{8,28},{12,24},{16,4},{20,0},{24,12},{28,8},{1,21},{... | collective-permute-start | bytes 442376 | tf_op jit(solution)/shard_map/ppermute | solution.py:187
  28.0 22.4 %collective-permute-start.6 = (f32[72,512]{1,0:T(8,128)S(1)}, f32[72,512]{1,0:T(8,128)S(1)}, u32[]{:S(2)}, u32[]{:S(2)}) collective-permute-start(f32[72,512]{1,0:T(8,128)S(1)} %get-tuple-element.18), channel_id=1, source_target_pairs={{0,16},{4,20},{8,24},{12,28},{16,0},{20,4},{24,8},{28,12},{1,17},{... | collective-permute-start | bytes 442376 | tf_op jit(solution)/shard_map/ppermute | solution.py:187
  30.1 20.4 %collective-permute-start.7 = (f32[72,512]{1,0:T(8,128)S(1)}, f32[72,512]{1,0:T(8,128)S(1)}, u32[]{:S(2)}, u32[]{:S(2)}) collective-permute-start(f32[72,512]{1,0:T(8,128)S(1)} %get-tuple-element.19), channel_id=1, source_target_pairs={{0,12},{4,8},{8,4},{12,0},{16,28},{20,24},{24,20},{28,16},{1,13},{... | collective-permute-start | bytes 442376 | tf_op jit(solution)/shard_map/ppermute | solution.py:187
  32.3 18.1 %collective-permute-start.8 = (f32[72,512]{1,0:T(8,128)S(1)}, f32[72,512]{1,0:T(8,128)S(1)}, u32[]{:S(2)}, u32[]{:S(2)}) collective-permute-start(f32[72,512]{1,0:T(8,128)S(1)} %get-tuple-element.20), channel_id=1, source_target_pairs={{0,8},{4,12},{8,0},{12,4},{16,24},{20,28},{24,16},{28,20},{1,9},{5... | collective-permute-start | bytes 442376 | tf_op jit(solution)/shard_map/ppermute | solution.py:187
  34.1 16.4 %collective-permute-start.9 = (f32[72,512]{1,0:T(8,128)S(1)}, f32[72,512]{1,0:T(8,128)S(1)}, u32[]{:S(2)}, u32[]{:S(2)}) collective-permute-start(f32[72,512]{1,0:T(8,128)S(1)} %get-tuple-element.21), channel_id=1, source_target_pairs={{0,4},{4,0},{8,12},{12,8},{16,20},{20,16},{24,28},{28,24},{1,5},{5... | collective-permute-start | bytes 442376 | tf_op jit(solution)/shard_map/ppermute | solution.py:187
  51.5 5.2 %collective-permute-start.12 = (f32[8,128]{1,0:T(8,128)S(1)}, f32[8,128]{1,0:T(8,128)S(1)}, u32[]{:S(2)}, u32[]{:S(2)}) collective-permute-start(f32[8,128]{1,0:T(8,128)S(1)} %get-tuple-element.23.rest_0_), channel_id=1, source_target_pairs={{0,3},{1,2},{2,1},{3,0},{4,7},{5,6},{6,5},{7,4},{8,11},{9,10},{10,... | collective-permute-start | bytes 12296 | tf_op jit(solution)/shard_map/ppermute | solution.py:187
  51.6 6.6 %collective-permute-start.11 = (f32[8,128]{1,0:T(8,128)S(1)}, f32[8,128]{1,0:T(8,128)S(1)}, u32[]{:S(2)}, u32[]{:S(2)}) collective-permute-start(f32[8,128]{1,0:T(8,128)S(1)} %get-tuple-element.23.rest_0_), channel_id=1, source_target_pairs={{0,2},{1,3},{2,0},{3,1},{4,6},{5,7},{6,4},{7,5},{8,10},{9,11},{10,... | collective-permute-start | bytes 12296 | tf_op jit(solution)/shard_map/ppermute | solution.py:187
  56.6 1.6 %collective-permute-start.10 = (f32[8,128]{1,0:T(8,128)S(1)}, f32[8,128]{1,0:T(8,128)S(1)}, u32[]{:S(2)}, u32[]{:S(2)}) collective-permute-start(f32[8,128]{1,0:T(8,128)S(1)} %get-tuple-element.23.rest_0_), channel_id=1, source_target_pairs={{0,1},{1,0},{2,3},{3,2},{4,5},{5,4},{6,7},{7,6},{8,9},{9,8},{10,11... | collective-permute-start | bytes 12296 | tf_op jit(solution)/shard_map/ppermute | solution.py:187

commit v2 on v0

v2 whole, which is shorter than its diff:
```python
import functools

import jax
import jax.numpy as jnp
from jax import lax
from jax.experimental import pallas as pl
from jax.experimental.pallas import tpu as pltpu
from jax.sharding import PartitionSpec as P

F32 = jnp.float32
BF16 = jnp.bfloat16
NN = (((1,), (0,)), ((), ()))
NT = (((1,), (1,)), ((), ()))
VMEM = pl.BlockSpec(memory_space=pltpu.VMEM)
HBM = pl.BlockSpec(memory_space=pltpu.HBM)
FAR_ROWS = (1, 1)
OWN, NEAR, FAR = 0, 1, 2
TAIL = 8


def split(value):
    high = value.astype(BF16)
    low = (value - high.astype(F32)).astype(BF16)
    return high, low


def product(left, right, dims):
    (lh, ll), (rh, rl) = left, right
    dot = functools.partial(lax.dot_general, dimension_numbers=dims, preferred_element_type=F32)
    return dot(lh, rh) + (dot(lh, rl) + dot(ll, rh))


def keep(value, rows, cols, first_row=0):
    col = lax.broadcasted_iota(jnp.int32, value.shape, 1)
    if rows is None:
        return jnp.where(col < cols, value, 0.0)
    row = lax.broadcasted_iota(jnp.int32, value.shape, 0) + first_row
    return jnp.where((row < rows) & (col < cols), value, 0.0)


def add_channels(kind, first, table, psi_ref, lh, ll, rh, rl, total, ph, pl_):
    rows = psi_ref.shape[0]
    chans = lh.shape[0]
    have = table[0, 6 + kind]
    listed = [table[0, 9 + kind * chans + i] for i in range(chans)]

    def channel(at):
        found = listed[0]
        for i in range(1, chans):
            found = jnp.where(at == i, listed[i], found)
        return found

    @pl.when(have > 0)
    def _():
        ph[:rows], pl_[:rows] = split(keep(psi_ref[...], table[0, 2 * kind], table[0, 2 * kind + 1], first))

        def group(start, size):
            ids = [channel(start + i) for i in range(size)]
            psi = (ph[:rows], pl_[:rows])
            ys = [split(product(psi, (rh[c], rl[c]), NT)) for c in ids]
            more = None
            for c, y in zip(ids, ys):
                lmat = (lh[c, :, pl.ds(first, rows)], ll[c, :, pl.ds(first, rows)])
                term = product(lmat, y, NN)
                more = term if more is None else more + term
            total[...] += more

        def pairs(i, carry):
            group(2 * i, 2)
            return carry

        if chans > 1:
            lax.fori_loop(0, have // 2, pairs, 0)

        @pl.when(lax.rem(have, 2) == 1)
        def _():
            group(have - 1, 1)


def prep_kernel(
    lsz, rsz, charge, state, left, right,
    table, psi, psi_band, norm, lh, ll, rh, rl,
    ls, rs, cs, lbuf, rbuf, sbuf, sems, more,
):
    chans = left.shape[0]
    me = lax.axis_index("narrow")
    count = ls.shape[0]
    small = [
        pltpu.make_async_copy(src, dst, more.at[i])
        for i, (src, dst) in enumerate(((lsz, ls), (rsz, rs), (charge, cs)))
    ]
    rights = [pltpu.make_async_copy(right.at[c, 0], rbuf.at[c], sems.at[0, c]) for c in range(chans)]
    lefts = [pltpu.make_async_copy(left.at[c, 0], lbuf.at[c], sems.at[1, c]) for c in range(chans)]
    whole = pltpu.make_async_copy(state.at[0], sbuf, more.at[3])
    for copy in small:
        copy.start()
    for c in range(chans):
        rights[c].start()
        lefts[c].start()
    whole.start()
    for copy in small:
        copy.wait()

    side = 1 - 2 * lax.rem(me, 2)
    sectors = (me, me + side, me - side)

    def size_at(sizes, sector):
        inside = (sector >= 0) & (sector < count)
        return jnp.where(inside, sizes[jnp.clip(sector, 0, count - 1)], 0)

    place = lax.broadcasted_iota(jnp.int32, table.shape, 1)
    entries = jnp.zeros(table.shape, jnp.int32)
    for kind, sector in enumerate(sectors):
        entries = jnp.where(place == 2 * kind, size_at(ls, sector), entries)
        entries = jnp.where(place == 2 * kind + 1, size_at(rs, sector), entries)
        have = 0
        for c in range(chans):
            src = me - (cs[c] - 1)
            match = (src == sector) & (sector >= 0) & (sector < count)
            entries = jnp.where(match & (place == 9 + kind * chans + have), c, entries)
            have += match.astype(jnp.int32)
        entries = jnp.where(place == 6 + kind, have, entries)
    table[...] = entries

    for c in range(chans):
        src = me - (cs[c] - 1)
        rights[c].wait()
        rh[c], rl[c] = split(keep(rbuf[c], None, size_at(rs, src)))
        lefts[c].wait()
        lh[c], ll[c] = split(keep(lbuf[c], None, size_at(ls, src)))

    whole.wait()
    masked = keep(sbuf[...], size_at(ls, me), size_at(rs, me))
    psi[...] = masked
    norm[...] = jnp.full(norm.shape, jnp.sum(masked * masked), F32)
    band = psi_band.shape[0]
    psi_band[...] = psi[pl.ds(pl.multiple_of(lax.axis_index("wide") * band, band), band), :]


def near_kernel(table, near, psi, lh, ll, rh, rl, total, ph, pl_):
    total[...] = jnp.zeros_like(total)
    add_channels(OWN, 0, table, psi, lh, ll, rh, rl, total, ph, pl_)
    add_channels(NEAR, 0, table, near, lh, ll, rh, rl, total, ph, pl_)


def far_kernel(first, table, psi_ref, lh, ll, rh, rl, before, total, ph, pl_):
    add_channels(FAR, first, table, psi_ref, lh, ll, rh, rl, total, ph, pl_)


def last_kernel(first, orders, table, psi_ref, lh, ll, rh, rl, before, psi, norm, *rest):
    *outs, total, ph, pl_ = rest
    total[...] = before[...]
    add_channels(FAR, first, table, psi_ref, lh, ll, rh, rl, total, ph, pl_)
    hpsi = keep(total[...], table[0, 0], table[0, 1])
    total[...] = hpsi
    numerator = jnp.sum(psi[...] * hpsi)
    here = lax.axis_index("wide")
    band = psi.shape[0] // lax.axis_size("wide")
    row = lax.broadcasted_iota(jnp.int32, (TAIL, psi.shape[1]), 0)
    sums = jnp.where(row == 0, numerator, norm[0, 0])
    for order, out in zip(orders, outs):
        for place, shift in enumerate(order):
            start = pl.multiple_of((here ^ shift) * band, band)
            out[place * band : (place + 1) * band, :] = total[pl.ds(start, band), :]
        if out.shape[0] > len(order) * band:
            out[len(order) * band :, :] = sums


def add_up(parts):
    parts = [part[...] for part in parts]
    whole = parts[0]
    for part in parts[1:]:
        whole += part
    tail = jnp.concatenate([whole[-TAIL : 1 - TAIL], parts[0][1 - TAIL :]], axis=0)
    return whole[:-TAIL], tail


def merge_kernel(*refs):
    *parts, mine, give = refs
    whole, sums = add_up(parts)
    half = mine.shape[0] - TAIL
    mine[:half, :] = whole[:half]
    give[:half, :] = whole[half:]
    mine[half:, :] = sums
    give[half:, :] = sums


def pass_kernel(*refs):
    *parts, out = refs
    whole, sums = add_up(parts)
    out[:-TAIL, :] = whole
    out[-TAIL:, :] = sums


def gather_kernel(n_plain, *refs):
    *parts, share, sums = refs
    whole, tail = add_up(parts[n_plain:])
    for part in parts[:n_plain]:
        whole += part[...]
    share[...] = whole
    sums[...] = tail[:, : sums.shape[1]]


def final_kernel(psi, share, *rest):
    *sums, out, alpha = rest
    both = sums[0][...]
    for more in sums[1:]:
        both += more[...]
    ratio = both[0:1, :] / both[1:2, :]
    out[...] = share[...] - jnp.concatenate([ratio] * (psi.shape[1] // ratio.shape[1]), axis=1) * psi[...]
    alpha[...] = ratio


def exchange(value, axis, shift):
    count = lax.axis_size(axis)
    return lax.ppermute(value, axis, [(i, i ^ shift) for i in range(count)])


def f32(*shape):
    return jax.ShapeDtypeStruct(shape, F32)


def call(kernel, out_shape, n_in, out_specs, scratch=(), limit=16, name=None, **more):
    return pl.pallas_call(
        kernel,
        out_shape=out_shape,
        in_specs=[VMEM] * n_in,
        out_specs=out_specs,
        scratch_shapes=scratch,
        compiler_params=pltpu.CompilerParams(vmem_limit_bytes=limit * 2**20),
        name=name,
        **more,
    )


def per_device(state, left_env, right_env, left_sizes, right_sizes, channel_charge):
    chans, _, block, _ = left_env.shape
    n_wide, n_narrow = lax.axis_size("wide"), lax.axis_size("narrow")
    band = block // n_wide
    own = state[0]

    ends = [(0, 0), (n_narrow - 1, n_narrow - 1)]
    across = [pair for k in range(1, n_narrow - 1, 2) for pair in ((k, k + 1), (k + 1, k))]
    cuts = [0]
    for share in FAR_ROWS:
        cuts.append(cuts[-1] + share * block // sum(FAR_ROWS))
    fars = [lax.ppermute(own[a:b], "narrow", across + ends) for a, b in zip(cuts, cuts[1:])]
    near = exchange(own, "narrow", 1)

    halves = jax.ShapeDtypeStruct((chans, block, block), BF16)
    table, psi, psi_band, norm, *envs = pl.pallas_call(
        prep_kernel,
        out_shape=[jax.ShapeDtypeStruct((8, 128), jnp.int32), f32(block, block), f32(band, block), f32(8, 128)]
        + [halves] * 4,
        in_specs=[HBM] * 6,
        out_specs=[VMEM] * 8,
        scratch_shapes=[
            pltpu.SMEM(left_sizes.shape, jnp.int32),
            pltpu.SMEM(right_sizes.shape, jnp.int32),
            pltpu.SMEM(channel_charge.shape, jnp.int32),
            pltpu.VMEM((chans, block, block), F32),
            pltpu.VMEM((chans, block, block), F32),
            pltpu.VMEM((block, block), F32),
            pltpu.SemaphoreType.DMA((2, chans)),
            pltpu.SemaphoreType.DMA((4,)),
        ],
        compiler_params=pltpu.CompilerParams(vmem_limit_bytes=32 * 2**20),
        name="prep",
    )(
        left_sizes, right_sizes, channel_charge,
        *(pltpu.with_memory_space_constraint(x, pltpu.HBM) for x in (state, left_env, right_env)),
    )

    square = f32(block, block)
    pair = [pltpu.VMEM((block, block), BF16)] * 2
    total = call(near_kernel, square, 7, VMEM, pair, name="near")(table, near, psi, *envs)
    for first, far in zip(cuts[:-2], fars[:-1]):
        total = call(
            functools.partial(far_kernel, first), square, 7, VMEM, pair, name="far", input_output_aliases={6: 0}
        )(table, far, *envs, total)

    def last(orders, shapes):
        return call(
            functools.partial(last_kernel, cuts[-2], orders),
            [f32(rows, block) for rows in shapes], 9, [VMEM] * len(orders),
            [pltpu.VMEM((block, block), F32)] + pair, name="last",
        )(table, fars[-1], *envs, total, psi, norm)

    groups = min(4, n_wide)
    held = n_wide // groups
    orders = [[s + groups * place for place in range(held)] for s in range(groups)]
    blocks = last(orders, [held * band + TAIL] * groups)
    plain = []
    parts = [blocks[0]] + [exchange(blocks[s], "wide", s) for s in range(groups - 1, 0, -1)]
    while held > 1:
        held //= 2
        mine, give = call(merge_kernel, [f32(held * band + TAIL, block)] * 2, len(parts), [VMEM] * 2, name="merge")(
            *parts
        )
        parts = [mine, exchange(give, "wide", groups * held)]

    share, sums = call(
        functools.partial(gather_kernel, len(plain)), [f32(band, block), f32(8, 128)], len(plain) + len(parts),
        [VMEM] * 2, name="gather",
    )(*plain, *parts)
    every = [sums] + [exchange(sums, "narrow", s) for s in range(1, n_narrow)]
    out, alpha = call(final_kernel, [f32(band, block), f32(1, 128)], 2 + len(every), [VMEM] * 2, name="final")(
        psi_band, share, *every
    )
    return out[None], alpha[0, 0]


def solution(mesh):
    placed = (
        P("narrow", None, None),
        P("wide", "narrow", None, None),
        P("wide", "narrow", None, None),
        P(),
        P(),
        P("wide"),
    )
    return jax.shard_map(
        per_device,
        mesh=mesh,
        in_specs=placed,
        out_specs=(P("narrow", "wide", None), P()),
        check_vma=False,
    )
```

time: 171 us -> 48.2 us (0.28)
  waiting for transfers between devices: 74.2 us -> 11.2 us
  blocking collectives: 40.2 us -> 0 us
  between operations: 19.2 us -> 0.77 us
  starting transfers between devices: 3.75 us -> 21.5 us
  matrix products: 16.6 us -> 0 us
  other arithmetic: 14.8 us -> 0 us
  Pallas kernels: 0 us -> 12.6 us
    reduce_scatter x1 -> x0, waiting for transfers between devices: 74.2 us -> none  [per_device(): share = lax.psum_scatter(terms, 'wide', scatter_dimension=1, tiled=True)]
    psum x1 -> x0, blocking collectives: 40.2 us -> none  [per_device(): lax.psum((numerator, denominator), ('wide', 'narrow'))]
    ppermute x2 -> x10, starting transfers between devices: 3.72 us -> 21.5 us  [the longest x8 20.2 us: exchange(): return lax.ppermute(value, axis, [(i, i ^ shift) for i in range(count)])]
    dot_general x8 -> x0, matrix products: 16.6 us -> none  [the longest x4 8.98 us: per_device(): jnp.dot(inners[item], rmats[item].T, precision=lax.Precision.HIGHEST)]
    pallas_call x0 -> x7, Pallas kernels: none -> 12.6 us  [the longest x1 6.5 us: per_device(): call(near_kernel, square, 7, VMEM, pair, name='near')]
    ppermute x2 -> x10, waiting for transfers between devices: 0.01 us -> 11.2 us  [the longest x8 11.2 us: exchange(): return lax.ppermute(value, axis, [(i, i ^ shift) for i in range(count)])]
    convert_element_type x10 -> x0, other arithmetic: 6.57 us -> none  [valid_vector(): return (positions < count).astype(jnp.float32)]
    reduce_sum x3 -> x0, other arithmetic: 4.82 us -> none  [the longest x1 1.68 us: per_device(): numerator = jnp.sum(psi_mine * share)]
  transfers between devices with their start and end apart: 3 -> 10, of which waited for: 1 -> 5; matrix products, arithmetic and copies ran while one was open for 4% -> 3% of each run, Pallas kernels for 0% -> 23%
where the time goes in v2:
time: 48.2 us; the launch traced here: 47.4 us
  starting transfers between devices  21.5 us (45%)
  Pallas kernels  12.6 us (26%)
  waiting for transfers between devices  11.2 us (23%)
  local copies, waits for them, and re-layouts  1.28 us (3%)
  between operations  0.77 us (2%)
    ppermute x8, starting transfers between devices, exchange(): return lax.ppermute(value, axis, [(i, i ^ shift) for i in range(count)])  20.2 us
    ppermute x8, waiting for transfers between devices, exchange(): return lax.ppermute(value, axis, [(i, i ^ shift) for i in range(count)])  11.2 us
    pallas_call x1, Pallas kernels, per_device(): call(near_kernel, square, 7, VMEM, pair, name='near')  6.5 us
    pallas_call x1, Pallas kernels, per_device(): pl.pallas_call(prep_kernel, out_shape=[jax.ShapeDtypeStruct((8, 128), jnp...  4.31 us
    ppermute x2, starting transfers between devices, per_device(): lax.ppermute(own[a:b], 'narrow', across + ends)  1.39 us
    slice x1, local copies, waits for them, and re-layouts, per_device(): own[a:b]  1.27 us
  transfers between devices with their start and end apart: 10, of which 5 were waited for; matrix products, arithmetic and copies ran while one was open for 3% of the time, Pallas kernels for 23%

profile of v2, /device:TPU:0, one launch (start us, length us, event | category | flops | bytes accessed | tf_op | source)
XLA Modules:
  0.0 47.4 jit_solution(6560401872301035374)
XLA Ops:
  0.6 0.0 copy-start.2
  0.6 0.0 copy-start.1
  0.7 0.0 copy-start
  0.7 0.5 %collective-permute-start.2 = (f32[512,512]{1,0:T(8,128)}, f32[512,512]{1,0:T(8,128)S(1)}, u32[]{:S(2)}, u32[]{:S(2)}) collective-permute-start(f32[512,512]{1,0:T(8,128)} %bitcast.8), channel_id=1, source_target_pairs={{0,1},{1,0},{2,3},{3,2},{4,5},{5,4},{6,7},{7,6},{8,9},{9,8},{10,11... | collective-permute-start | bytes 3145736 | tf_op jit(solution)/shard_map/ppermute | solution.py:216
  1.2 1.3 %slice_bitcast_fusion = (f32[256,512]{1,0:T(8,128)S(1)}, f32[256,512]{1,0:T(8,128)S(1)}) fusion(f32[1,512,512]{2,1,0:T(8,128)} %state.1), kind=kLoop, calls=%fused_computation | loop fusion | bytes 2097152 | tf_op jit(solution)/shard_map/slice | solution.py:247
  2.4 0.7 %collective-permute-start.1 = (f32[256,512]{1,0:T(8,128)S(1)}, f32[256,512]{1,0:T(8,128)S(1)}, u32[]{:S(2)}, u32[]{:S(2)}) collective-permute-start(f32[256,512]{1,0:T(8,128)S(1)} %get-tuple-element.38), channel_id=1, source_target_pairs={{1,2},{2,1},{0,0},{3,3},{5,6},{6,5},{4,4},{7,7},{9,10},{10,9},{8,8... | collective-permute-start | bytes 1572872 | tf_op jit(solution)/shard_map/ppermute | solution.py:247
  3.2 0.7 %collective-permute-start = (f32[256,512]{1,0:T(8,128)S(1)}, f32[256,512]{1,0:T(8,128)S(1)}, u32[]{:S(2)}, u32[]{:S(2)}) collective-permute-start(f32[256,512]{1,0:T(8,128)S(1)} %get-tuple-element.39), channel_id=1, source_target_pairs={{1,2},{2,1},{0,0},{3,3},{5,6},{6,5},{4,4},{7,7},{9,10},{10,9},{8,8... | collective-permute-start | bytes 1572872 | tf_op jit(solution)/shard_map/ppermute | solution.py:247
  3.9 0.0 copy-done.2
  3.9 0.0 copy-done.1
  3.9 0.0 copy-done
  3.9 4.3 %prep.1 = (s32[8,128]{1,0:T(8,128)S(1)}, f32[512,512]{1,0:T(8,128)S(1)}, f32[64,512]{1,0:T(8,128)S(1)}, f32[8,128]{1,0:T(8,128)S(1)}, bf16[4,512,512]{2,1,0:T(8,...) custom-call(s32[4]{0:T(128)S(1)} %copy-done, ...), custom_call_target="tpu_custom_call" | custom-call | tf_op jit(solution)/shard_map/prep/pallas_call | solution.py:251
  8.2 0.0 collective-permute-done.2.near
  8.2 6.5 %near.1.before = f32[512,512]{1,0:T(8,128)S(1)} custom-call(s32[8,128]{1,0:T(8,128)S(1)} %get-tuple-element.21.table, f32[512,512]{1,0:T(8,128)S(1)} %collective-permute-done.2.near, f32[512,512]{1,0:T(8,128)S(1)} %get-tuple-element.26.psi, bf16[4,512,512]{2,1,0:T(8,128)(2,1)S(1)} %get-tuple-element.22.lh, bf16[4,512,512]{2,1,0:T(8,128)(2,1)S(1)} %get-tuple-element.23.ll, ...), custom_call_target="tpu_custom_call" | custom-call | tf_op jit(solution)/shard_map/near/pallas_call | solution.py:276
  14.7 0.0 collective-permute-done.1.psi_ref
  14.7 0.3 far.1.before
  15.0 0.0 collective-permute-done.psi_ref
  15.0 0.7 %last.1 = (f32[136,512]{1,0:T(8,128)S(1)}, f32[136,512]{1,0:T(8,128)S(1)}, f32[136,512]{1,0:T(8,128)S(1)}, f32[136,512]{1,0:T(8,128)S(1)}) custom-call(s32[8,128]{1,0:T(8,128)S(1)} %get-tuple-element.21.table, f32[256,512]{1,0:T(8,128)S(1)} %collective-permute-done.psi_ref, bf16[4,512,512]{2,1,0:T(8,128)(2,1)S(1)} %get-tuple-element.22.lh, ...), custom_call_target="tpu_custom_call" | custom-call | tf_op jit(solution)/shard_map/last/pallas_call | solution.py:283
  15.8 1.2 %collective-permute-start.3 = (f32[136,512]{1,0:T(8,128)S(1)}, f32[136,512]{1,0:T(8,128)S(1)}, u32[]{:S(2)}, u32[]{:S(2)}) collective-permute-start(f32[136,512]{1,0:T(8,128)S(1)} %get-tuple-element.29), channel_id=1, source_target_pairs={{0,12},{4,8},{8,4},{12,0},{16,28},{20,24},{24,20},{28,16},{1,13},{... | collective-permute-start | bytes 835592 | tf_op jit(solution)/shard_map/ppermute | solution.py:216
  17.0 1.5 %collective-permute-start.4 = (f32[136,512]{1,0:T(8,128)S(1)}, f32[136,512]{1,0:T(8,128)S(1)}, u32[]{:S(2)}, u32[]{:S(2)}) collective-permute-start(f32[136,512]{1,0:T(8,128)S(1)} %get-tuple-element.30), channel_id=1, source_target_pairs={{0,8},{4,12},{8,0},{12,4},{16,24},{20,28},{24,16},{28,20},{1,9},{5... | collective-permute-start | bytes 835592 | tf_op jit(solution)/shard_map/ppermute | solution.py:216
  18.5 1.4 %collective-permute-start.5 = (f32[136,512]{1,0:T(8,128)S(1)}, f32[136,512]{1,0:T(8,128)S(1)}, u32[]{:S(2)}, u32[]{:S(2)}) collective-permute-start(f32[136,512]{1,0:T(8,128)S(1)} %get-tuple-element.31), channel_id=1, source_target_pairs={{0,4},{4,0},{8,12},{12,8},{16,20},{20,16},{24,28},{28,24},{1,5},{5... | collective-permute-start | bytes 835592 | tf_op jit(solution)/shard_map/ppermute | solution.py:216
  19.9 3.5 %collective-permute-done.3.refs_1_ = f32[136,512]{1,0:T(8,128)S(1)} collective-permute-done((f32[136,512]{1,0:T(8,128)S(1)}, f32[136,512]{1,0:T(8,128)S(1)}, u32[]{:S(2)}, u32[]{:S(2)}) %collective-permute-start.3) | collective-permute-done | bytes 278560 | tf_op jit(solution)/shard_map/ppermute | solution.py:216
  23.4 2.5 %collective-permute-done.4.refs_2_ = f32[136,512]{1,0:T(8,128)S(1)} collective-permute-done((f32[136,512]{1,0:T(8,128)S(1)}, f32[136,512]{1,0:T(8,128)S(1)}, u32[]{:S(2)}, u32[]{:S(2)}) %collective-permute-start.4) | collective-permute-done | bytes 278560 | tf_op jit(solution)/shard_map/ppermute | solution.py:216
  26.0 0.3 collective-permute-done.5.refs_3_
  26.3 0.1 merge.1
  26.4 3.9 %collective-permute-start.6 = (f32[72,512]{1,0:T(8,128)S(1)}, f32[72,512]{1,0:T(8,128)S(1)}, u32[]{:S(2)}, u32[]{:S(2)}) collective-permute-start(f32[72,512]{1,0:T(8,128)S(1)} %get-tuple-element.33), channel_id=1, source_target_pairs={{0,16},{4,20},{8,24},{12,28},{16,0},{20,4},{24,8},{28,12},{1,17},{... | collective-permute-start | bytes 442376 | tf_op jit(solution)/shard_map/ppermute | solution.py:216
  30.3 3.3 %collective-permute-done.6.refs_1_ = f32[72,512]{1,0:T(8,128)S(1)} collective-permute-done((f32[72,512]{1,0:T(8,128)S(1)}, f32[72,512]{1,0:T(8,128)S(1)}, u32[]{:S(2)}, u32[]{:S(2)}) %collective-permute-start.6) | collective-permute-done | bytes 147488 | tf_op jit(solution)/shard_map/ppermute | solution.py:216
  33.6 2.8 %collective-permute-start.9 = (f32[8,128]{1,0:T(8,128)S(1)}, f32[8,128]{1,0:T(8,128)S(1)}, u32[]{:S(2)}, u32[]{:S(2)}) collective-permute-start(f32[8,128]{1,0:T(8,128)S(1)} %get-tuple-element.35.rest_0_), channel_id=1, source_target_pairs={{0,3},{1,2},{2,1},{3,0},{4,7},{5,6},{6,5},{7,4},{8,11},{9,10},{10,... | collective-permute-start | bytes 12296 | tf_op jit(solution)/shard_map/ppermute | solution.py:216
  36.4 8.7 %collective-permute-start.8 = (f32[8,128]{1,0:T(8,128)S(1)}, f32[8,128]{1,0:T(8,128)S(1)}, u32[]{:S(2)}, u32[]{:S(2)}) collective-permute-start(f32[8,128]{1,0:T(8,128)S(1)} %get-tuple-element.35.rest_0_), channel_id=1, source_target_pairs={{0,2},{1,3},{2,0},{3,1},{4,6},{5,7},{6,4},{7,5},{8,10},{9,11},{10,... | collective-permute-start | bytes 12296 | tf_op jit(solution)/shard_map/ppermute | solution.py:216
  45.2 0.0 collective-permute-start.7
  45.2 0.0 collective-permute-done.9.rest_3_
  45.2 1.5 %collective-permute-done.8.rest_2_ = f32[8,128]{1,0:T(8,128)S(1)} collective-permute-done((f32[8,128]{1,0:T(8,128)S(1)}, f32[8,128]{1,0:T(8,128)S(1)}, u32[]{:S(2)}, u32[]{:S(2)}) %collective-permute-start.8) | collective-permute-done | bytes 4128 | tf_op jit(solution)/shard_map/ppermute | solution.py:216
  46.7 0.0 collective-permute-done.7.rest_1_
  46.7 0.7 %final.1 = (f32[64,512]{1,0:T(8,128)}, f32[1,128]{1,0:T(1,128)}) custom-call(f32[64,512]{1,0:T(8,128)S(1)} %get-tuple-element.20.psi, f32[64,512]{1,0:T(8,128)S(1)} %get-tuple-element.34.share, f32[8,128]{1,0:T(8,128)S(1)} %get-tuple-element.35.rest_0_, f32[8,128]{1,0:T(8,128)S(1)} %collective-permute-done.7.rest_1_, ...), custom_call_target="tpu_custom_call" | custom-call | tf_op jit(solution)/shard_map/final/pallas_call | solution.py:307
  (1 shorter events, 0.0 us)
Async XLA Ops:
  0.6 3.2 %copy-start.2 = (s32[4]{0:T(128)S(1)}, s32[4]{0:T(128)}, u32[]{:S(2)}) copy-start(s32[4]{0:T(128)} %charge.1) | copy-start | bytes 52
  0.6 3.2 %copy-start.1 = (s32[4]{0:T(128)S(1)}, s32[4]{0:T(128)}, u32[]{:S(2)}) copy-start(s32[4]{0:T(128)} %rsz.1) | copy-start | bytes 52
  0.7 3.2 %copy-start = (s32[4]{0:T(128)S(1)}, s32[4]{0:T(128)}, u32[]{:S(2)}) copy-start(s32[4]{0:T(128)} %lsz.1) | copy-start | bytes 52
  0.7 7.5 %collective-permute-start.2 = (f32[512,512]{1,0:T(8,128)}, f32[512,512]{1,0:T(8,128)S(1)}, u32[]{:S(2)}, u32[]{:S(2)}) collective-permute-start(f32[512,512]{1,0:T(8,128)} %bitcast.8), channel_id=1, source_target_pairs={{0,1},{1,0},{2,3},{3,2},{4,5},{5,4},{6,7},{7,6},{8,9},{9,8},{10,11... | collective-permute-start | bytes 3145736 | tf_op jit(solution)/shard_map/ppermute | solution.py:216
  2.4 12.3 %collective-permute-start.1 = (f32[256,512]{1,0:T(8,128)S(1)}, f32[256,512]{1,0:T(8,128)S(1)}, u32[]{:S(2)}, u32[]{:S(2)}) collective-permute-start(f32[256,512]{1,0:T(8,128)S(1)} %get-tuple-element.38), channel_id=1, source_target_pairs={{1,2},{2,1},{0,0},{3,3},{5,6},{6,5},{4,4},{7,7},{9,10},{10,9},{8,8... | collective-permute-start | bytes 1572872 | tf_op jit(solution)/shard_map/ppermute | solution.py:247
  3.2 11.9 %collective-permute-start = (f32[256,512]{1,0:T(8,128)S(1)}, f32[256,512]{1,0:T(8,128)S(1)}, u32[]{:S(2)}, u32[]{:S(2)}) collective-permute-start(f32[256,512]{1,0:T(8,128)S(1)} %get-tuple-element.39), channel_id=1, source_target_pairs={{1,2},{2,1},{0,0},{3,3},{5,6},{6,5},{4,4},{7,7},{9,10},{10,9},{8,8... | collective-permute-start | bytes 1572872 | tf_op jit(solution)/shard_map/ppermute | solution.py:247
  15.8 7.6 %collective-permute-start.3 = (f32[136,512]{1,0:T(8,128)S(1)}, f32[136,512]{1,0:T(8,128)S(1)}, u32[]{:S(2)}, u32[]{:S(2)}) collective-permute-start(f32[136,512]{1,0:T(8,128)S(1)} %get-tuple-element.29), channel_id=1, source_target_pairs={{0,12},{4,8},{8,4},{12,0},{16,28},{20,24},{24,20},{28,16},{1,13},{... | collective-permute-start | bytes 835592 | tf_op jit(solution)/shard_map/ppermute | solution.py:216
  17.0 8.9 %collective-permute-start.4 = (f32[136,512]{1,0:T(8,128)S(1)}, f32[136,512]{1,0:T(8,128)S(1)}, u32[]{:S(2)}, u32[]{:S(2)}) collective-permute-start(f32[136,512]{1,0:T(8,128)S(1)} %get-tuple-element.30), channel_id=1, source_target_pairs={{0,8},{4,12},{8,0},{12,4},{16,24},{20,28},{24,16},{28,20},{1,9},{5... | collective-permute-start | bytes 835592 | tf_op jit(solution)/shard_map/ppermute | solution.py:216
  18.5 7.8 %collective-permute-start.5 = (f32[136,512]{1,0:T(8,128)S(1)}, f32[136,512]{1,0:T(8,128)S(1)}, u32[]{:S(2)}, u32[]{:S(2)}) collective-permute-start(f32[136,512]{1,0:T(8,128)S(1)} %get-tuple-element.31), channel_id=1, source_target_pairs={{0,4},{4,0},{8,12},{12,8},{16,20},{20,16},{24,28},{28,24},{1,5},{5... | collective-permute-start | bytes 835592 | tf_op jit(solution)/shard_map/ppermute | solution.py:216
  26.4 7.2 %collective-permute-start.6 = (f32[72,512]{1,0:T(8,128)S(1)}, f32[72,512]{1,0:T(8,128)S(1)}, u32[]{:S(2)}, u32[]{:S(2)}) collective-permute-start(f32[72,512]{1,0:T(8,128)S(1)} %get-tuple-element.33), channel_id=1, source_target_pairs={{0,16},{4,20},{8,24},{12,28},{16,0},{20,4},{24,8},{28,12},{1,17},{... | collective-permute-start | bytes 442376 | tf_op jit(solution)/shard_map/ppermute | solution.py:216
  33.6 11.6 %collective-permute-start.9 = (f32[8,128]{1,0:T(8,128)S(1)}, f32[8,128]{1,0:T(8,128)S(1)}, u32[]{:S(2)}, u32[]{:S(2)}) collective-permute-start(f32[8,128]{1,0:T(8,128)S(1)} %get-tuple-element.35.rest_0_), channel_id=1, source_target_pairs={{0,3},{1,2},{2,1},{3,0},{4,7},{5,6},{6,5},{7,4},{8,11},{9,10},{10,... | collective-permute-start | bytes 12296 | tf_op jit(solution)/shard_map/ppermute | solution.py:216
  36.4 10.3 %collective-permute-start.8 = (f32[8,128]{1,0:T(8,128)S(1)}, f32[8,128]{1,0:T(8,128)S(1)}, u32[]{:S(2)}, u32[]{:S(2)}) collective-permute-start(f32[8,128]{1,0:T(8,128)S(1)} %get-tuple-element.35.rest_0_), channel_id=1, source_target_pairs={{0,2},{1,3},{2,0},{3,1},{4,6},{5,7},{6,4},{7,5},{8,10},{9,11},{10,... | collective-permute-start | bytes 12296 | tf_op jit(solution)/shard_map/ppermute | solution.py:216
  45.2 1.6 %collective-permute-start.7 = (f32[8,128]{1,0:T(8,128)S(1)}, f32[8,128]{1,0:T(8,128)S(1)}, u32[]{:S(2)}, u32[]{:S(2)}) collective-permute-start(f32[8,128]{1,0:T(8,128)S(1)} %get-tuple-element.35.rest_0_), channel_id=1, source_target_pairs={{0,1},{1,0},{2,3},{3,2},{4,5},{5,4},{6,7},{7,6},{8,9},{9,8},{10,11... | collective-permute-start | bytes 12296 | tf_op jit(solution)/shard_map/ppermute | solution.py:216

commit v3 on v0

v3 whole, which is shorter than its diff:
```python
import functools

import jax
import jax.numpy as jnp
from jax import lax
from jax.experimental import pallas as pl
from jax.experimental.pallas import tpu as pltpu
from jax.sharding import PartitionSpec as P

F32 = jnp.float32
BF16 = jnp.bfloat16
NN = (((1,), (0,)), ((), ()))
NT = (((1,), (1,)), ((), ()))
VMEM = pl.BlockSpec(memory_space=pltpu.VMEM)
HBM = pl.BlockSpec(memory_space=pltpu.HBM)
OWN, NEAR, FAR, NONE = range(4)


def split(value):
    high = value.astype(BF16)
    low = (value - high.astype(F32)).astype(BF16)
    return high, low


def product(left, right, dims):
    (lh, ll), (rh, rl) = left, right
    dot = functools.partial(lax.dot_general, dimension_numbers=dims, preferred_element_type=F32)
    return dot(lh, rh) + (dot(lh, rl) + dot(ll, rh))


def keep(value, rows, cols, first_row=0):
    row = lax.broadcasted_iota(jnp.int32, value.shape, 0) + first_row
    col = lax.broadcasted_iota(jnp.int32, value.shape, 1)
    return jnp.where((row < rows) & (col < cols), value, 0.0)


def band_order(n_wide):
    groups = min(4, n_wide)
    return [s + groups * t for s in range(groups) for t in range(n_wide // groups)]


def main_kernel(
    lsz, rsz, charge, state, left, right, near,
    table, psi, psi_band, norm, lh, ll, rh, rl, total,
    ls, rs, cs, lbuf, rbuf, sbuf, ph, pl_, sems, more,
):
    chans, block = left.shape[0], state.shape[1]
    me, here = lax.axis_index("narrow"), lax.axis_index("wide")
    count = ls.shape[0]
    small = [
        pltpu.make_async_copy(src, dst, more.at[i])
        for i, (src, dst) in enumerate(((lsz, ls), (rsz, rs), (charge, cs)))
    ]
    whole = pltpu.make_async_copy(state.at[0], sbuf, more.at[3])
    for copy in small + [whole]:
        copy.start()
    for copy in small:
        copy.wait()

    side = 1 - 2 * lax.rem(me, 2)
    sectors = (me, me + side, me - side)

    def size_at(sizes, sector):
        inside = (sector >= 0) & (sector < count)
        return jnp.where(inside, sizes[jnp.clip(sector, 0, count - 1)], 0)

    lcounts = [size_at(ls, sector) for sector in sectors] + [0]
    rcounts = [size_at(rs, sector) for sector in sectors] + [0]

    def pick(values, kind):
        found = values[NONE]
        for i in (OWN, NEAR, FAR):
            found = jnp.where(kind == i, values[i], found)
        return found

    kinds = []
    for c in range(chans):
        src = me - (cs[c] - 1)
        kind = jnp.where(src == me, OWN, jnp.where(src == sectors[NEAR], NEAR, FAR))
        kinds.append(jnp.where((src >= 0) & (src < count), kind, NONE))
    places = [
        sum((kinds[o] < kinds[c]).astype(jnp.int32) for o in range(chans))
        + sum((kinds[o] == kinds[c]).astype(jnp.int32) for o in range(c))
        for c in range(chans)
    ]
    copies = []
    for j in range(chans):
        chan = sum(jnp.where(places[c] == j, c, 0) for c in range(chans))
        copies.append(
            (
                pltpu.make_async_copy(right.at[chan, 0], rbuf.at[j], sems.at[0, j]),
                pltpu.make_async_copy(left.at[chan, 0], lbuf.at[j], sems.at[1, j]),
            )
        )
        for copy in copies[-1]:
            copy.start()

    n_close = sum((k <= NEAR).astype(jnp.int32) for k in kinds)
    n_far = sum((k == FAR).astype(jnp.int32) for k in kinds)
    place = lax.broadcasted_iota(jnp.int32, table.shape, 1)
    entries = jnp.where(place == 0, lcounts[FAR], jnp.where(place == 1, rcounts[FAR], 0))
    table[...] = jnp.where(place == 2, n_close, jnp.where(place == 3, n_close + n_far, entries))

    order = band_order(lax.axis_size("wide"))
    band = psi_band.shape[0]
    starts = [pl.multiple_of((here ^ shift) * band, band) for shift in order]

    total[...] = jnp.zeros_like(total)
    ph[NEAR], pl_[NEAR] = split(keep(near[...], lcounts[NEAR], rcounts[NEAR]))
    whole.wait()
    masked = keep(sbuf[...], lcounts[OWN], rcounts[OWN])
    ph[OWN], pl_[OWN] = split(masked)
    norm[...] = jnp.full(norm.shape, jnp.sum(masked * masked), F32)
    sbuf[...] = masked
    psi_band[...] = sbuf[pl.ds(pl.multiple_of(here * band, band), band), :]
    for p, start in enumerate(starts):
        psi[p * band : (p + 1) * band, :] = sbuf[pl.ds(start, band), :]

    for j in range(chans):
        kind = sum(jnp.where(places[c] == j, kinds[c], 0) for c in range(chans))
        lcount, rcount = pick(lcounts, kind), pick(rcounts, kind)
        for copy in copies[j]:
            copy.wait()

        def halve():
            rh[j], rl[j] = split(keep(rbuf[j], rcounts[OWN], rcount))
            for p, start in enumerate(starts):
                rows = slice(p * band, (p + 1) * band)
                piece = keep(lbuf[j, pl.ds(start, band), :], lcounts[OWN], lcount, start)
                lh[j, rows, :], ll[j, rows, :] = split(piece)

        @pl.when(kind <= NEAR)
        def _():
            halve()
            y = split(product((ph[kind], pl_[kind]), (rh[j], rl[j]), NT))
            total[...] += product((lh[j], ll[j]), y, NN)

        @pl.when(kind > NEAR)
        def _():
            halve()


def over_far(table, chans, group):
    first, have = table[0, 2], table[0, 3] - table[0, 2]
    for count in range(1, chans + 1):

        @pl.when(have == count)
        def _():
            group([first + i for i in range(count)])


def far_kernel(table, far, lh, ll, rh, rl, before, total, ph, pl_):
    rows = far.shape[0]

    @pl.when(table[0, 3] > table[0, 2])
    def _():
        ph[...], pl_[...] = split(keep(far[...], table[0, 0], table[0, 1]))

        def group(slots):
            psi = (ph[...], pl_[...])
            ys = [split(product(psi, (rh[j], rl[j]), NT)) for j in slots]
            terms = [product((lh[j, :, :rows], ll[j, :, :rows]), y, NN) for j, y in zip(slots, ys)]
            total[...] += functools.reduce(jnp.add, terms)

        over_far(table, lh.shape[0], group)


def last_kernel(table, far, lh, ll, rh, rl, before, psi, norm, sums, *rest):
    *outs, total, ph, pl_ = rest
    rows = far.shape[0]
    block = psi.shape[0]
    total[...] = before[...]

    @pl.when(table[0, 3] > table[0, 2])
    def _():
        ph[...], pl_[...] = split(keep(far[...], table[0, 0], table[0, 1], block - rows))

        def group(slots):
            psi_far = (ph[...], pl_[...])
            ys = [split(product(psi_far, (rh[j], rl[j]), NT)) for j in slots]
            terms = [
                product((lh[j, :, block - rows :], ll[j, :, block - rows :]), y, NN) for j, y in zip(slots, ys)
            ]
            total[...] += functools.reduce(jnp.add, terms)

        over_far(table, lh.shape[0], group)

    row = lax.broadcasted_iota(jnp.int32, sums.shape, 0)
    sums[...] = jnp.where(row == 0, jnp.sum(psi[...] * total[...]), norm[...])
    size = outs[0].shape[0]
    for i, out in enumerate(outs):
        out[...] = total[i * size : (i + 1) * size, :]


def add_kernel(*refs):
    *parts, out = refs
    whole = parts[0][...]
    for part in parts[1:]:
        whole += part[...]
    out[...] = whole


def add_first_kernel(*refs):
    *parts, out = refs
    whole = parts[0][...]
    for part in parts[1:]:
        whole += part[...]
    row = lax.broadcasted_iota(jnp.int32, out.shape, 0)
    out[...] = jnp.where(row == 0, whole, parts[0][...])


def merge_kernel(_, *refs):
    *parts, mine, give = refs
    whole = parts[0][...]
    for part in parts[1:]:
        whole += part[...]
    half = mine.shape[0]
    mine[...] = whole[:half]
    give[...] = whole[half:]


def final_kernel(n_parts, psi, *rest):
    parts, (*sums, out, alpha) = rest[:n_parts], rest[n_parts:]
    numerator = sums[0][0:1, :]
    for more in sums[1:]:
        numerator += more[0:1, :]
    ratio = numerator / sums[0][1:2, :]
    share = parts[0][...]
    for part in parts[1:]:
        share += part[...]
    out[...] = share - jnp.concatenate([ratio] * (psi.shape[1] // ratio.shape[1]), axis=1) * psi[...]
    alpha[...] = ratio


def exchange(value, axis, shift):
    count = lax.axis_size(axis)
    return lax.ppermute(value, axis, [(i, i ^ shift) for i in range(count)])


def f32(*shape):
    return jax.ShapeDtypeStruct(shape, F32)


def cost(flops, size=2**20):
    return pl.CostEstimate(flops=flops, bytes_accessed=size, transcendentals=0)


def call(kernel, out_shape, n_in, scratch=(), name=None, **more):
    return pl.pallas_call(
        kernel,
        out_shape=out_shape,
        in_specs=[VMEM] * n_in,
        out_specs=jax.tree.map(lambda _: VMEM, out_shape),
        scratch_shapes=scratch,
        compiler_params=pltpu.CompilerParams(vmem_limit_bytes=16 * 2**20),
        name=name,
        **more,
    )


def per_device(state, left_env, right_env, left_sizes, right_sizes, channel_charge):
    chans, _, block, _ = left_env.shape
    n_wide, n_narrow = lax.axis_size("wide"), lax.axis_size("narrow")
    band, half = block // n_wide, block // 2
    own = state[0]
    square, small = f32(block, block), f32(8, 128)
    work = 6 * chans * block**3

    ends = [(0, 0), (n_narrow - 1, n_narrow - 1)]
    across = [pair for k in range(1, n_narrow - 1, 2) for pair in ((k, k + 1), (k + 1, k))]
    far_top, far_low = (lax.ppermute(rows, "narrow", across + ends) for rows in (own[:half], own[half:]))
    near = exchange(own, "narrow", 1)

    halves = jax.ShapeDtypeStruct((chans, block, block), BF16)
    table, psi, psi_band, norm, lh, ll, rh, rl, total = pl.pallas_call(
        main_kernel,
        out_shape=[jax.ShapeDtypeStruct((8, 128), jnp.int32), square, f32(band, block), small]
        + [halves] * 4
        + [square],
        in_specs=[HBM] * 6 + [VMEM],
        out_specs=[VMEM] * 9,
        scratch_shapes=[
            pltpu.SMEM(left_sizes.shape, jnp.int32),
            pltpu.SMEM(right_sizes.shape, jnp.int32),
            pltpu.SMEM(channel_charge.shape, jnp.int32),
            pltpu.VMEM((chans, block, block), F32),
            pltpu.VMEM((chans, block, block), F32),
            pltpu.VMEM((block, block), F32),
            pltpu.VMEM((2, block, block), BF16),
            pltpu.VMEM((2, block, block), BF16),
            pltpu.SemaphoreType.DMA((2, chans)),
            pltpu.SemaphoreType.DMA((4,)),
        ],
        compiler_params=pltpu.CompilerParams(vmem_limit_bytes=32 * 2**20),
        cost_estimate=cost(work, 8 * chans * block * block),
        name="main",
    )(
        left_sizes, right_sizes, channel_charge,
        *(pltpu.with_memory_space_constraint(x, pltpu.HBM) for x in (state, left_env, right_env)),
        near,
    )
    envs = (lh, ll, rh, rl)

    pair = [pltpu.VMEM((half, block), BF16)] * 2
    total = call(far_kernel, square, 7, pair, name="far", cost_estimate=cost(work), input_output_aliases={6: 0})(table, far_top, *envs, total)

    groups = min(4, n_wide)
    held = n_wide // groups
    sums, *blocks = call(
        last_kernel, [small] + [f32(held * band, block)] * groups, 9, [pltpu.VMEM((block, block), F32)] + pair,
        name="last", cost_estimate=cost(work),
    )(table, far_low, *envs, total, psi, norm)
    parts = [blocks[0]] + [exchange(blocks[s], "wide", s) for s in range(groups - 1, 0, -1)]

    if n_narrow <= 4:
        every = [exchange(sums, "narrow", s) for s in range(n_narrow - 1, 0, -1)]
        sums = call(add_kernel, small, n_narrow, name="sectors")(sums, *every)
    else:
        step = 1
        while step < n_narrow:
            sums = call(add_kernel, small, 2, name="sectors")(sums, exchange(sums, "narrow", step))
            step *= 2
    sums = call(add_first_kernel, small, 2, name="pair")(sums, exchange(sums, "wide", 1))
    others = [exchange(sums, "wide", s) for s in range(n_wide - 2, 0, -2)]
    while held > 1:
        held //= 2
        mine, give = call(merge_kernel, [f32(held * band, block)] * 2, 1 + len(parts), name="merge")(sums, *parts)
        parts = [mine, exchange(give, "wide", groups * held)]

    out, alpha = call(
        functools.partial(final_kernel, len(parts)), [f32(band, block), f32(1, 128)], 2 + len(parts) + len(others),
        name="final",
    )(psi_band, *parts, sums, *others)
    return out[None], alpha[0, 0]


def solution(mesh):
    placed = (
        P("narrow", None, None),
        P("wide", "narrow", None, None),
        P("wide", "narrow", None, None),
        P(),
        P(),
        P("wide"),
    )
    return jax.shard_map(
        per_device,
        mesh=mesh,
        in_specs=placed,
        out_specs=(P("narrow", "wide", None), P()),
        check_vma=False,
    )
```

time: 171 us -> 44.8 us (0.26)
  waiting for transfers between devices: 74.2 us -> 7.09 us
  blocking collectives: 40.2 us -> 0 us
  starting transfers between devices: 3.75 us -> 23.3 us
  between operations: 19.2 us -> 0.78 us
  matrix products: 16.6 us -> 0 us
  other arithmetic: 14.8 us -> 0 us
  Pallas kernels: 0 us -> 12 us
    reduce_scatter x1 -> x0, waiting for transfers between devices: 74.2 us -> none  [per_device(): share = lax.psum_scatter(terms, 'wide', scatter_dimension=1, tiled=True)]
    psum x1 -> x0, blocking collectives: 40.2 us -> none  [per_device(): lax.psum((numerator, denominator), ('wide', 'narrow'))]
    ppermute x2 -> x14, starting transfers between devices: 3.72 us -> 23.3 us  [the longest x12 21.9 us: exchange(): return lax.ppermute(value, axis, [(i, i ^ shift) for i in range(count)])]
    dot_general x8 -> x0, matrix products: 16.6 us -> none  [the longest x4 8.98 us: per_device(): jnp.dot(inners[item], rmats[item].T, precision=lax.Precision.HIGHEST)]
    pallas_call x0 -> x7, Pallas kernels: none -> 12 us  [the longest x1 10.4 us: per_device(): pl.pallas_call(main_kernel, out_shape=[jax.ShapeDtypeStruct((8, 128), jnp...]
    ppermute x2 -> x14, waiting for transfers between devices: 0.01 us -> 7.09 us  [the longest x12 7.08 us: exchange(): return lax.ppermute(value, axis, [(i, i ^ shift) for i in range(count)])]
    convert_element_type x10 -> x0, other arithmetic: 6.57 us -> none  [valid_vector(): return (positions < count).astype(jnp.float32)]
    reduce_sum x3 -> x0, other arithmetic: 4.82 us -> none  [the longest x1 1.68 us: per_device(): numerator = jnp.sum(psi_mine * share)]
  transfers between devices with their start and end apart: 3 -> 14, of which waited for: 1 -> 5; matrix products, arithmetic and copies ran while one was open for 4% -> 3% of each run, Pallas kernels for 0% -> 24%
where the time goes in v3:
time: 44.8 us; the launch traced here: 44.5 us
  starting transfers between devices  23.3 us (52%)
  Pallas kernels  12 us (27%)
  waiting for transfers between devices  7.09 us (16%)
  local copies, waits for them, and re-layouts  1.28 us (3%)
  between operations  0.78 us (2%)
    ppermute x12, starting transfers between devices, exchange(): return lax.ppermute(value, axis, [(i, i ^ shift) for i in range(count)])  21.9 us
    pallas_call x1, Pallas kernels, per_device(): pl.pallas_call(main_kernel, out_shape=[jax.ShapeDtypeStruct((8, 128), jnp...  10.4 us
    ppermute x12, waiting for transfers between devices, exchange(): return lax.ppermute(value, axis, [(i, i ^ shift) for i in range(count)])  7.08 us
    ppermute x2, starting transfers between devices, per_device(): lax.ppermute(rows, 'narrow', across + ends)  1.39 us
    slice x1, local copies, waits for them, and re-layouts, per_device(): own[:half]  1.27 us
  transfers between devices with their start and end apart: 14, of which 5 were waited for; matrix products, arithmetic and copies ran while one was open for 3% of the time, Pallas kernels for 24%

profile of v3, /device:TPU:0, one launch (start us, length us, event | category | flops | bytes accessed | tf_op | source)
XLA Modules:
  0.0 44.5 jit_solution(13675226187663709676)
XLA Ops:
  0.6 0.0 copy-start.2
  0.6 0.0 copy-start.1
  0.7 0.0 copy-start
  0.7 0.5 %collective-permute-start = (f32[512,512]{1,0:T(8,128)}, f32[512,512]{1,0:T(8,128)S(1)}, u32[]{:S(2)}, u32[]{:S(2)}) collective-permute-start(f32[512,512]{1,0:T(8,128)} %bitcast.8), channel_id=1, source_target_pairs={{0,1},{1,0},{2,3},{3,2},{4,5},{5,4},{6,7},{7,6},{8,9},{9,8},{10,11... | collective-permute-start | bytes 3145736 | tf_op jit(solution)/shard_map/ppermute | solution.py:237
  1.2 1.3 %slice_bitcast_fusion = (f32[256,512]{1,0:T(8,128)S(1)}, f32[256,512]{1,0:T(8,128)S(1)}) fusion(f32[1,512,512]{2,1,0:T(8,128)} %state.1), kind=kLoop, calls=%fused_computation | loop fusion | bytes 2097152 | tf_op jit(solution)/shard_map/slice | solution.py:271
  2.4 0.7 %collective-permute-start.2 = (f32[256,512]{1,0:T(8,128)S(1)}, f32[256,512]{1,0:T(8,128)S(1)}, u32[]{:S(2)}, u32[]{:S(2)}) collective-permute-start(f32[256,512]{1,0:T(8,128)S(1)} %get-tuple-element.38), channel_id=1, source_target_pairs={{1,2},{2,1},{0,0},{3,3},{5,6},{6,5},{4,4},{7,7},{9,10},{10,9},{8,8... | collective-permute-start | bytes 1572872 | tf_op jit(solution)/shard_map/ppermute | solution.py:271
  3.2 0.7 %collective-permute-start.1 = (f32[256,512]{1,0:T(8,128)S(1)}, f32[256,512]{1,0:T(8,128)S(1)}, u32[]{:S(2)}, u32[]{:S(2)}) collective-permute-start(f32[256,512]{1,0:T(8,128)S(1)} %get-tuple-element.39), channel_id=1, source_target_pairs={{1,2},{2,1},{0,0},{3,3},{5,6},{6,5},{4,4},{7,7},{9,10},{10,9},{8,8... | collective-permute-start | bytes 1572872 | tf_op jit(solution)/shard_map/ppermute | solution.py:271
  3.9 0.0 collective-permute-done.near
  3.9 0.0 copy-done.2
  3.9 0.0 copy-done.1
  3.9 0.0 copy-done
  3.9 10.4 %main.1 = (s32[8,128]{1,0:T(8,128)S(1)}, f32[512,512]{1,0:T(8,128)S(1)}, f32[64,512]{1,0:T(8,128)S(1)}, f32[8,128]{1,0:T(8,128)S(1)}, bf16[4,512,512]{2,1,0:T(8,...) custom-call(s32[4]{0:T(128)S(1)} %copy-done, ...), custom_call_target="tpu_custom_call" | custom-call | flops 3221225472 | bytes 8388608 | tf_op jit(solution)/shard_map/main/pallas_call | solution.py:275
  14.3 0.0 collective-permute-done.2.far
  14.3 0.3 far.1.before
  14.7 0.0 collective-permute-done.1.far
  14.7 0.5 %last.1 = (f32[8,128]{1,0:T(8,128)S(1)}, f32[128,512]{1,0:T(8,128)S(1)}, f32[128,512]{1,0:T(8,128)S(1)}, f32[128,512]{1,0:T(8,128)S(1)}, f32[128,512]{1,0:T(8,128)S(1)}) custom-call(s32[8,128]{1,0:T(8,128)S(1)} %get-tuple-element.21.table, f32[256,512]{1,0:T(8,128)S(1)} %collective-permute-done.1.far, bf16[4,512,512]{2,1,0:T(8,128)(2,1)S(1)} %get-tuple-element.22.lh, ...), custom_call_target="tpu_custom_call" | custom-call | flops 3221225472 | bytes 1048576 | tf_op jit(solution)/shard_map/last/pallas_call | solution.py:309
  15.2 0.6 %collective-permute-start.7 = (f32[128,512]{1,0:T(8,128)S(1)}, f32[128,512]{1,0:T(8,128)S(1)}, u32[]{:S(2)}, u32[]{:S(2)}) collective-permute-start(f32[128,512]{1,0:T(8,128)S(1)} %get-tuple-element.31), channel_id=1, source_target_pairs={{0,12},{4,8},{8,4},{12,0},{16,28},{20,24},{24,20},{28,16},{1,13},{... | collective-permute-start | bytes 786440 | tf_op jit(solution)/shard_map/ppermute | solution.py:237
  15.8 2.0 %collective-permute-start.8 = (f32[128,512]{1,0:T(8,128)S(1)}, f32[128,512]{1,0:T(8,128)S(1)}, u32[]{:S(2)}, u32[]{:S(2)}) collective-permute-start(f32[128,512]{1,0:T(8,128)S(1)} %get-tuple-element.32), channel_id=1, source_target_pairs={{0,8},{4,12},{8,0},{12,4},{16,24},{20,28},{24,16},{28,20},{1,9},{5... | collective-permute-start | bytes 786440 | tf_op jit(solution)/shard_map/ppermute | solution.py:237
  17.8 0.9 %collective-permute-start.9 = (f32[128,512]{1,0:T(8,128)S(1)}, f32[128,512]{1,0:T(8,128)S(1)}, u32[]{:S(2)}, u32[]{:S(2)}) collective-permute-start(f32[128,512]{1,0:T(8,128)S(1)} %get-tuple-element.33), channel_id=1, source_target_pairs={{0,4},{4,0},{8,12},{12,8},{16,20},{20,16},{24,28},{28,24},{1,5},{5... | collective-permute-start | bytes 786440 | tf_op jit(solution)/shard_map/ppermute | solution.py:237
  18.7 6.8 %collective-permute-start.5 = (f32[8,128]{1,0:T(8,128)S(1)}, f32[8,128]{1,0:T(8,128)S(1)}, u32[]{:S(2)}, u32[]{:S(2)}) collective-permute-start(f32[8,128]{1,0:T(8,128)S(1)} %get-tuple-element.29.refs_0_), channel_id=1, source_target_pairs={{0,1},{1,0},{2,3},{3,2},{4,5},{5,4},{6,7},{7,6},{8,9},{9,8},{10,11... | collective-permute-start | bytes 12296 | tf_op jit(solution)/shard_map/ppermute | solution.py:237
  25.5 1.4 %collective-permute-start.4 = (f32[8,128]{1,0:T(8,128)S(1)}, f32[8,128]{1,0:T(8,128)S(1)}, u32[]{:S(2)}, u32[]{:S(2)}) collective-permute-start(f32[8,128]{1,0:T(8,128)S(1)} %get-tuple-element.29.refs_0_), channel_id=1, source_target_pairs={{0,2},{1,3},{2,0},{3,1},{4,6},{5,7},{6,4},{7,5},{8,10},{9,11},{10,... | collective-permute-start | bytes 12296 | tf_op jit(solution)/shard_map/ppermute | solution.py:237
  26.9 0.0 collective-permute-done.5.refs_3_
  26.9 0.9 %collective-permute-start.3 = (f32[8,128]{1,0:T(8,128)S(1)}, f32[8,128]{1,0:T(8,128)S(1)}, u32[]{:S(2)}, u32[]{:S(2)}) collective-permute-start(f32[8,128]{1,0:T(8,128)S(1)} %get-tuple-element.29.refs_0_), channel_id=1, source_target_pairs={{0,3},{1,2},{2,1},{3,0},{4,7},{5,6},{6,5},{7,4},{8,11},{9,10},{10,... | collective-permute-start | bytes 12296 | tf_op jit(solution)/shard_map/ppermute | solution.py:237
  27.9 1.3 %collective-permute-done.4.refs_2_ = f32[8,128]{1,0:T(8,128)S(1)} collective-permute-done((f32[8,128]{1,0:T(8,128)S(1)}, f32[8,128]{1,0:T(8,128)S(1)}, u32[]{:S(2)}, u32[]{:S(2)}) %collective-permute-start.4) | collective-permute-done | bytes 4128 | tf_op jit(solution)/shard_map/ppermute | solution.py:237
  29.1 0.8 %collective-permute-done.3.refs_1_ = f32[8,128]{1,0:T(8,128)S(1)} collective-permute-done((f32[8,128]{1,0:T(8,128)S(1)}, f32[8,128]{1,0:T(8,128)S(1)}, u32[]{:S(2)}, u32[]{:S(2)}) %collective-permute-start.3) | collective-permute-done | bytes 4128 | tf_op jit(solution)/shard_map/ppermute | solution.py:237
  30.0 1.5 %collective-permute-start.6 = (f32[8,128]{1,0:T(8,128)S(1)}, f32[8,128]{1,0:T(8,128)S(1)}, u32[]{:S(2)}, u32[]{:S(2)}) collective-permute-start(f32[8,128]{1,0:T(8,128)S(1)} %sectors.1.refs_0_), channel_id=1, source_target_pairs={{0,4},{4,0},{8,12},{12,8},{16,20},{20,16},{24,28},{28,24},{1,5},{5... | collective-permute-start | bytes 12296 | tf_op jit(solution)/shard_map/ppermute | solution.py:237
  31.4 2.1 %collective-permute-done.6.refs_1_ = f32[8,128]{1,0:T(8,128)S(1)} collective-permute-done((f32[8,128]{1,0:T(8,128)S(1)}, f32[8,128]{1,0:T(8,128)S(1)}, u32[]{:S(2)}, u32[]{:S(2)}) %collective-permute-start.6) | collective-permute-done | bytes 4128 | tf_op jit(solution)/shard_map/ppermute | solution.py:237
  33.6 0.0 collective-permute-done.7.refs_1_
  33.6 0.0 collective-permute-done.8.refs_2_
  33.6 0.0 collective-permute-done.9.refs_3_
  33.6 0.1 merge.1
  33.7 2.9 %collective-permute-start.10 = (f32[64,512]{1,0:T(8,128)S(1)}, f32[64,512]{1,0:T(8,128)S(1)}, u32[]{:S(2)}, u32[]{:S(2)}) collective-permute-start(f32[64,512]{1,0:T(8,128)S(1)} %get-tuple-element.35), channel_id=1, source_target_pairs={{0,16},{4,20},{8,24},{12,28},{16,0},{20,4},{24,8},{28,12},{1,17},{... | collective-permute-start | bytes 393224 | tf_op jit(solution)/shard_map/ppermute | solution.py:237
  36.6 1.7 %collective-permute-start.13 = (f32[8,128]{1,0:T(8,128)S(1)}, f32[8,128]{1,0:T(8,128)S(1)}, u32[]{:S(2)}, u32[]{:S(2)}) collective-permute-start(f32[8,128]{1,0:T(8,128)S(1)} %pair.1._.rest_2_), channel_id=1, source_target_pairs={{0,8},{4,12},{8,0},{12,4},{16,24},{20,28},{24,16},{28,20},{1,9},{5... | collective-permute-start | bytes 12296 | tf_op jit(solution)/shard_map/ppermute | solution.py:237
  38.3 0.1 collective-permute-start.12
  38.4 2.6 %collective-permute-start.11 = (f32[8,128]{1,0:T(8,128)S(1)}, f32[8,128]{1,0:T(8,128)S(1)}, u32[]{:S(2)}, u32[]{:S(2)}) collective-permute-start(f32[8,128]{1,0:T(8,128)S(1)} %pair.1._.rest_2_), channel_id=1, source_target_pairs={{0,24},{4,28},{8,16},{12,20},{16,8},{20,12},{24,0},{28,4},{1,25},{... | collective-permute-start | bytes 12296 | tf_op jit(solution)/shard_map/ppermute | solution.py:237
  41.0 0.0 collective-permute-done.13.rest_5_
  41.0 1.9 %collective-permute-done.12.rest_4_ = f32[8,128]{1,0:T(8,128)S(1)} collective-permute-done((f32[8,128]{1,0:T(8,128)S(1)}, f32[8,128]{1,0:T(8,128)S(1)}, u32[]{:S(2)}, u32[]{:S(2)}) %collective-permute-start.12) | collective-permute-done | bytes 4128 | tf_op jit(solution)/shard_map/ppermute | solution.py:237
  42.8 1.0 %collective-permute-done.11.rest_3_ = f32[8,128]{1,0:T(8,128)S(1)} collective-permute-done((f32[8,128]{1,0:T(8,128)S(1)}, f32[8,128]{1,0:T(8,128)S(1)}, u32[]{:S(2)}, u32[]{:S(2)}) %collective-permute-start.11) | collective-permute-done | bytes 4128 | tf_op jit(solution)/shard_map/ppermute | solution.py:237
  43.8 0.0 collective-permute-done.10.rest_1_
  43.8 0.7 %final.1 = (f32[64,512]{1,0:T(8,128)}, f32[1,128]{1,0:T(1,128)}) custom-call(f32[64,512]{1,0:T(8,128)S(1)} %get-tuple-element.20.psi, f32[64,512]{1,0:T(8,128)S(1)} %get-tuple-element.34.rest_0_, f32[64,512]{1,0:T(8,128)S(1)} %collective-permute-done.10.rest_1_, f32[8,128]{1,0:T(8,128)S(1)} %pair.1._.rest_2_, f32[8,128]{1,0:T(8,128)S(1)} %collective-permute-done.11.rest_3_, ...), custom_call_target="tpu_custom_call" | custom-call | tf_op jit(solution)/shard_map/final/pallas_call | solution.py:330
  (2 shorter events, 0.0 us)
Async XLA Ops:
  0.6 3.2 %copy-start.2 = (s32[4]{0:T(128)S(1)}, s32[4]{0:T(128)}, u32[]{:S(2)}) copy-start(s32[4]{0:T(128)} %charge.1) | copy-start | bytes 52
  0.6 3.2 %copy-start.1 = (s32[4]{0:T(128)S(1)}, s32[4]{0:T(128)}, u32[]{:S(2)}) copy-start(s32[4]{0:T(128)} %rsz.1) | copy-start | bytes 52
  0.7 3.2 %copy-start = (s32[4]{0:T(128)S(1)}, s32[4]{0:T(128)}, u32[]{:S(2)}) copy-start(s32[4]{0:T(128)} %lsz.1) | copy-start | bytes 52
  0.7 3.2 %collective-permute-start = (f32[512,512]{1,0:T(8,128)}, f32[512,512]{1,0:T(8,128)S(1)}, u32[]{:S(2)}, u32[]{:S(2)}) collective-permute-start(f32[512,512]{1,0:T(8,128)} %bitcast.8), channel_id=1, source_target_pairs={{0,1},{1,0},{2,3},{3,2},{4,5},{5,4},{6,7},{7,6},{8,9},{9,8},{10,11... | collective-permute-start | bytes 3145736 | tf_op jit(solution)/shard_map/ppermute | solution.py:237
  2.4 11.9 %collective-permute-start.2 = (f32[256,512]{1,0:T(8,128)S(1)}, f32[256,512]{1,0:T(8,128)S(1)}, u32[]{:S(2)}, u32[]{:S(2)}) collective-permute-start(f32[256,512]{1,0:T(8,128)S(1)} %get-tuple-element.38), channel_id=1, source_target_pairs={{1,2},{2,1},{0,0},{3,3},{5,6},{6,5},{4,4},{7,7},{9,10},{10,9},{8,8... | collective-permute-start | bytes 1572872 | tf_op jit(solution)/shard_map/ppermute | solution.py:271
  3.2 11.5 %collective-permute-start.1 = (f32[256,512]{1,0:T(8,128)S(1)}, f32[256,512]{1,0:T(8,128)S(1)}, u32[]{:S(2)}, u32[]{:S(2)}) collective-permute-start(f32[256,512]{1,0:T(8,128)S(1)} %get-tuple-element.39), channel_id=1, source_target_pairs={{1,2},{2,1},{0,0},{3,3},{5,6},{6,5},{4,4},{7,7},{9,10},{10,9},{8,8... | collective-permute-start | bytes 1572872 | tf_op jit(solution)/shard_map/ppermute | solution.py:271
  15.2 18.4 %collective-permute-start.7 = (f32[128,512]{1,0:T(8,128)S(1)}, f32[128,512]{1,0:T(8,128)S(1)}, u32[]{:S(2)}, u32[]{:S(2)}) collective-permute-start(f32[128,512]{1,0:T(8,128)S(1)} %get-tuple-element.31), channel_id=1, source_target_pairs={{0,12},{4,8},{8,4},{12,0},{16,28},{20,24},{24,20},{28,16},{1,13},{... | collective-permute-start | bytes 786440 | tf_op jit(solution)/shard_map/ppermute | solution.py:237
  15.8 17.8 %collective-permute-start.8 = (f32[128,512]{1,0:T(8,128)S(1)}, f32[128,512]{1,0:T(8,128)S(1)}, u32[]{:S(2)}, u32[]{:S(2)}) collective-permute-start(f32[128,512]{1,0:T(8,128)S(1)} %get-tuple-element.32), channel_id=1, source_target_pairs={{0,8},{4,12},{8,0},{12,4},{16,24},{20,28},{24,16},{28,20},{1,9},{5... | collective-permute-start | bytes 786440 | tf_op jit(solution)/shard_map/ppermute | solution.py:237
  17.8 15.8 %collective-permute-start.9 = (f32[128,512]{1,0:T(8,128)S(1)}, f32[128,512]{1,0:T(8,128)S(1)}, u32[]{:S(2)}, u32[]{:S(2)}) collective-permute-start(f32[128,512]{1,0:T(8,128)S(1)} %get-tuple-element.33), channel_id=1, source_target_pairs={{0,4},{4,0},{8,12},{12,8},{16,20},{20,16},{24,28},{28,24},{1,5},{5... | collective-permute-start | bytes 786440 | tf_op jit(solution)/shard_map/ppermute | solution.py:237
  18.7 8.2 %collective-permute-start.5 = (f32[8,128]{1,0:T(8,128)S(1)}, f32[8,128]{1,0:T(8,128)S(1)}, u32[]{:S(2)}, u32[]{:S(2)}) collective-permute-start(f32[8,128]{1,0:T(8,128)S(1)} %get-tuple-element.29.refs_0_), channel_id=1, source_target_pairs={{0,1},{1,0},{2,3},{3,2},{4,5},{5,4},{6,7},{7,6},{8,9},{9,8},{10,11... | collective-permute-start | bytes 12296 | tf_op jit(solution)/shard_map/ppermute | solution.py:237
  25.5 3.6 %collective-permute-start.4 = (f32[8,128]{1,0:T(8,128)S(1)}, f32[8,128]{1,0:T(8,128)S(1)}, u32[]{:S(2)}, u32[]{:S(2)}) collective-permute-start(f32[8,128]{1,0:T(8,128)S(1)} %get-tuple-element.29.refs_0_), channel_id=1, source_target_pairs={{0,2},{1,3},{2,0},{3,1},{4,6},{5,7},{6,4},{7,5},{8,10},{9,11},{10,... | collective-permute-start | bytes 12296 | tf_op jit(solution)/shard_map/ppermute | solution.py:237
  26.9 3.0 %collective-permute-start.3 = (f32[8,128]{1,0:T(8,128)S(1)}, f32[8,128]{1,0:T(8,128)S(1)}, u32[]{:S(2)}, u32[]{:S(2)}) collective-permute-start(f32[8,128]{1,0:T(8,128)S(1)} %get-tuple-element.29.refs_0_), channel_id=1, source_target_pairs={{0,3},{1,2},{2,1},{3,0},{4,7},{5,6},{6,5},{7,4},{8,11},{9,10},{10,... | collective-permute-start | bytes 12296 | tf_op jit(solution)/shard_map/ppermute | solution.py:237
  30.0 3.6 %collective-permute-start.6 = (f32[8,128]{1,0:T(8,128)S(1)}, f32[8,128]{1,0:T(8,128)S(1)}, u32[]{:S(2)}, u32[]{:S(2)}) collective-permute-start(f32[8,128]{1,0:T(8,128)S(1)} %sectors.1.refs_0_), channel_id=1, source_target_pairs={{0,4},{4,0},{8,12},{12,8},{16,20},{20,16},{24,28},{28,24},{1,5},{5... | collective-permute-start | bytes 12296 | tf_op jit(solution)/shard_map/ppermute | solution.py:237
  33.7 10.1 %collective-permute-start.10 = (f32[64,512]{1,0:T(8,128)S(1)}, f32[64,512]{1,0:T(8,128)S(1)}, u32[]{:S(2)}, u32[]{:S(2)}) collective-permute-start(f32[64,512]{1,0:T(8,128)S(1)} %get-tuple-element.35), channel_id=1, source_target_pairs={{0,16},{4,20},{8,24},{12,28},{16,0},{20,4},{24,8},{28,12},{1,17},{... | collective-permute-start | bytes 393224 | tf_op jit(solution)/shard_map/ppermute | solution.py:237
  36.6 4.4 %collective-permute-start.13 = (f32[8,128]{1,0:T(8,128)S(1)}, f32[8,128]{1,0:T(8,128)S(1)}, u32[]{:S(2)}, u32[]{:S(2)}) collective-permute-start(f32[8,128]{1,0:T(8,128)S(1)} %pair.1._.rest_2_), channel_id=1, source_target_pairs={{0,8},{4,12},{8,0},{12,4},{16,24},{20,28},{24,16},{28,20},{1,9},{5... | collective-permute-start | bytes 12296 | tf_op jit(solution)/shard_map/ppermute | solution.py:237
  38.3 4.5 %collective-permute-start.12 = (f32[8,128]{1,0:T(8,128)S(1)}, f32[8,128]{1,0:T(8,128)S(1)}, u32[]{:S(2)}, u32[]{:S(2)}) collective-permute-start(f32[8,128]{1,0:T(8,128)S(1)} %pair.1._.rest_2_), channel_id=1, source_target_pairs={{0,16},{4,20},{8,24},{12,28},{16,0},{20,4},{24,8},{28,12},{1,17},{... | collective-permute-start | bytes 12296 | tf_op jit(solution)/shard_map/ppermute | solution.py:237
  38.4 5.4 %collective-permute-start.11 = (f32[8,128]{1,0:T(8,128)S(1)}, f32[8,128]{1,0:T(8,128)S(1)}, u32[]{:S(2)}, u32[]{:S(2)}) collective-permute-start(f32[8,128]{1,0:T(8,128)S(1)} %pair.1._.rest_2_), channel_id=1, source_target_pairs={{0,24},{4,28},{8,16},{12,20},{16,8},{20,12},{24,0},{28,4},{1,25},{... | collective-permute-start | bytes 12296 | tf_op jit(solution)/shard_map/ppermute | solution.py:237
